TPU v7x, 256 devices: a whole 4x4x8 slice. The times are simulated.
256 devices in a mesh: ctx: 32 (over x, z), tp: 8 (over y, core).
Axes of the slice: x: 4, y: 4, z: 8, core: 2. Of those that a mesh axis runs over, the one named last changes fastest.
Arguments:
- queries: bfloat16 [16384, 4096], P('ctx', 'tp'), may hold values from -6 to 6
- prefix_kv: bfloat16 [2, 65536, 1024], P(None, 'ctx', 'tp'), may hold values from -6 to 6
- fresh_kv: bfloat16 [2, 16384, 1024], P(None, 'ctx', 'tp'), may hold values from -6 to 6
- group_blocks: int32 [8, 16], replicated, may hold values from 0 to 639, as said below
- head_pick: int32 [32, 16], replicated, may hold values 0 or 1
- band_start: int32 [32, 4], replicated, may hold values from 0 to 1280, as said below
- band_width: int32 [32, 4], replicated, may hold values from 1 to 256
- o_weight: bfloat16 [4096, 4096], P('tp'), may hold values from -0.125 to 0.125
Outputs:
- projected: bfloat16 [16384, 4096], P('ctx', 'tp')
Inputs may be any that keep to these rules, and one draw needn't show every extreme that they name: `group_blocks`: within a row the 16 blocks are distinct; column 0 is block 0 in every row. `band_start`: column 0 is 0 in every row.
All inputs are finite; a program needn't handle non-finite values.
Results may differ from a plain program's by a relative error of at most 0.017.
Values may be sent and summed in bfloat16 or wider, within the bound.
A program may use at most 64 MiB of HBM per device.

v0:
```python
import math

import jax
import jax.numpy as jnp
from jax import lax
from jax.sharding import PartitionSpec as P

QH = 32
KVH = 8
HD = 128
BLK = 128
NG = 16
NS = 4


def passed_along(block, axis, distance):
    devices = range(lax.axis_size(axis))
    route = [(i - distance, i) for i in devices if i - distance in devices]
    return lax.ppermute(block, axis, route)


def local(queries, prefix_kv, fresh_kv, group_blocks, head_pick, band_start, band_width, o_weight):
    tok_rows = fresh_kv.shape[1]
    prefix_rows = prefix_kv.shape[1]
    local_groups = fresh_kv.shape[2] // HD
    per_group = QH // KVH
    local_heads = local_groups * per_group
    ctx_size = lax.axis_size("ctx")
    ctx_index = lax.axis_index("ctx")
    tp_index = lax.axis_index("tp")
    prefix_len = prefix_rows * ctx_size
    score_scale = 1.0 / math.sqrt(HD)
    group_ids = tp_index * local_groups + jnp.arange(local_groups, dtype=jnp.int32)
    head_ids = tp_index * local_heads + jnp.arange(local_heads, dtype=jnp.int32)
    blocks = jnp.take(group_blocks, group_ids, axis=0)
    head_picks = jnp.take(head_pick, head_ids, axis=0) == 1
    starts = jnp.take(band_start, head_ids, axis=0)
    widths = jnp.take(band_width, head_ids, axis=0)
    local_kv = jnp.concatenate([prefix_kv, fresh_kv], axis=1).reshape(
        2, prefix_rows + tok_rows, local_groups, HD
    )
    first_pos = blocks * BLK
    in_prefix = first_pos < prefix_len
    fresh_first = first_pos - prefix_len
    offset = jnp.where(
        in_prefix,
        first_pos - ctx_index * prefix_rows,
        prefix_rows + fresh_first - ctx_index * tok_rows,
    )
    is_owned = jnp.where(
        in_prefix,
        (first_pos >= ctx_index * prefix_rows) & (first_pos < (ctx_index + 1) * prefix_rows),
        (fresh_first >= ctx_index * tok_rows) & (fresh_first < (ctx_index + 1) * tok_rows),
    )
    row_index = (
        jnp.clip(offset, 0, prefix_rows + tok_rows - BLK)[:, :, None]
        + jnp.arange(BLK, dtype=jnp.int32)[None, None, :]
    ).reshape(local_groups, NG * BLK)
    picked = jnp.stack([local_kv[:, row_index[0], 0, :]], axis=1)
    slot_owned = jnp.repeat(is_owned, BLK, axis=1)
    picked = jnp.where(slot_owned[None, :, :, None], picked, jnp.zeros((), picked.dtype))
    slot_pick = jnp.repeat(head_picks, BLK, axis=1)
    head_group_local = jnp.arange(local_heads, dtype=jnp.int32) // per_group
    per_head_kv = jnp.where(
        slot_pick[None, :, :, None], picked[:, head_group_local], jnp.zeros((), picked.dtype)
    )
    vert_kv = lax.psum(per_head_kv, "ctx").astype(jnp.float32).astype(jnp.bfloat16)
    earlier = [passed_along(fresh_kv, "ctx", reach_back) for reach_back in (3, 2, 1)]
    window = jnp.concatenate(earlier + [fresh_kv], axis=1).reshape(
        2, 4 * tok_rows, local_groups, HD
    )
    query_pos = prefix_len + ctx_index * tok_rows + jnp.arange(tok_rows, dtype=jnp.int32)
    window_pos = prefix_len + (ctx_index - 3) * tok_rows + jnp.arange(4 * tok_rows, dtype=jnp.int32)
    window_block = window_pos // BLK
    fresh_key = window_pos >= prefix_len
    distance = query_pos[:, None] - window_pos[None, :]
    query_heads = queries.reshape(tok_rows, local_heads, HD)
    slot_pos = (first_pos[:, :, None] + jnp.arange(BLK, dtype=jnp.int32)[None, None, :]).reshape(
        local_groups, NG * BLK
    )
    contract = (((1,), (1,)), ((), ()))

    def attend_head(head_index):
        local_group = head_index // per_group
        query_rows = lax.dynamic_index_in_dim(query_heads, head_index, 1, keepdims=False)
        vert_keys = lax.dynamic_index_in_dim(vert_kv[0], head_index, 0, keepdims=False)
        vert_values = lax.dynamic_index_in_dim(vert_kv[1], head_index, 0, keepdims=False)
        band_keys = lax.dynamic_index_in_dim(window[0], local_group, 1, keepdims=False)
        band_values = lax.dynamic_index_in_dim(window[1], local_group, 1, keepdims=False)
        pick_row = lax.dynamic_index_in_dim(head_picks, head_index, 0, keepdims=False)
        slot_pick_row = lax.dynamic_index_in_dim(slot_pick, head_index, 0, keepdims=False)
        slot_row = lax.dynamic_index_in_dim(slot_pos, local_group, 0, keepdims=False)
        block_row = lax.dynamic_index_in_dim(blocks, local_group, 0, keepdims=False)
        start_row = lax.dynamic_index_in_dim(starts, head_index, 0, keepdims=False)
        width_row = lax.dynamic_index_in_dim(widths, head_index, 0, keepdims=False)
        vert_mask = slot_pick_row[None, :] & (slot_row[None, :] <= query_pos[:, None])
        in_vert = jnp.any((window_block[:, None] == block_row[None, :]) & pick_row[None, :], axis=1)
        in_band = jnp.zeros(distance.shape, jnp.bool_)
        for band_index in range(NS):
            in_band = in_band | (distance >= start_row[band_index]) & (
                distance < start_row[band_index] + width_row[band_index]
            )
        band_mask = (
            in_band & jnp.logical_not(in_vert)[None, :] & (distance >= 0) & fresh_key[None, :]
        )
        vert_scores = (
            lax.dot_general(query_rows, vert_keys, contract, preferred_element_type=jnp.float32)
            * score_scale
        )
        band_scores = (
            lax.dot_general(query_rows, band_keys, contract, preferred_element_type=jnp.float32)
            * score_scale
        )
        row_max = jnp.maximum(
            jnp.max(jnp.where(vert_mask, vert_scores, -jnp.inf), axis=1, keepdims=True),
            jnp.max(jnp.where(band_mask, band_scores, -jnp.inf), axis=1, keepdims=True),
        )
        vert_exp = jnp.where(vert_mask, jnp.exp(vert_scores - row_max), 0.0)
        band_exp = jnp.where(band_mask, jnp.exp(band_scores - row_max), 0.0)
        row_total = jnp.sum(vert_exp, axis=1, keepdims=True) + jnp.sum(
            band_exp, axis=1, keepdims=True
        )
        vert_probs = (vert_exp / row_total).astype(jnp.bfloat16)
        band_probs = (band_exp / row_total).astype(jnp.bfloat16)
        head_out = jnp.dot(vert_probs, vert_values, preferred_element_type=jnp.float32)
        head_out = head_out + jnp.dot(band_probs, band_values, preferred_element_type=jnp.float32)
        return head_out.astype(jnp.bfloat16)

    attended = lax.map(attend_head, jnp.arange(local_heads, dtype=jnp.int32))
    attended_rows = attended.transpose(1, 0, 2).reshape(tok_rows, local_heads * HD)
    projected = jnp.dot(attended_rows, o_weight, preferred_element_type=jnp.float32)
    return lax.psum_scatter(projected.astype(jnp.bfloat16), "tp", scatter_dimension=1, tiled=True)


def solution(mesh):
    return jax.shard_map(
        local,
        mesh=mesh,
        in_specs=(
            P("ctx", "tp"),
            P(None, "ctx", "tp"),
            P(None, "ctx", "tp"),
            P(),
            P(),
            P(),
            P(),
            P("tp", None),
        ),
        out_specs=P("ctx", "tp"),
        check_vma=False,
    )
```

profile of v0, /device:TPU:1, one launch (start us, length us, event | category | flops | bytes accessed | tf_op | source)
XLA Modules:
  0.0 426.2 jit_solution(13987883502820506635)
XLA Ops:
  10.1 2.8 copy.32
  13.1 10.8 %maximum_bitcast_fusion = bf16[2,2560,1,128]{3,0,2,1:T(2,128)(2,1)S(1)} fusion(bf16[2,512,128]{2,0,1:T(2,128)(2,1)S(1)} %copy.33, bf16[2,2048,128]{2,0,1:T(2,128)(2,1)S(1)} %copy.32), kind=kLoop, calls=%fused_computation.85 | loop fusion | flops 655360 | bytes 2621440 | tf_op jit(solution)/shard_map/reshape | solution.py:39
  23.9 7.2 %gather_fusion.1 = bf16[2048,2,128]{2,1,0:T(2,128)(2,1)S(1)} fusion(bf16[2,2560,1,128]{3,0,2,1:T(2,128)(2,1)S(1)} %maximum_bitcast_fusion, s32[2048]{0:T(1024)S(1)} %bitcast.128), kind=kCustom, calls=%fused_computation.3 | custom fusion | bytes 2113536 | tf_op jit(solution)/shard_map/gather | solution.py:59
  31.1 7.5 %fusion.54 = bf16[2,2048,128]{2,0,1:T(2,128)(2,1)S(1)} fusion(bf16[2048,2,128]{2,1,0:T(2,128)(2,1)S(1)} %gather_fusion.1, pred[2048]{0:T(1024)(128)(4,1)S(1)} %broadcast_bitcast_fusion.1), kind=kLoop, calls=%fused_computation.87 | loop fusion | flops 524288 | bytes 2099200 | tf_op jit(solution)/shard_map/gather | solution.py:65
  38.8 4.1 broadcast_select_fusion
  42.9 5.7 %collective-permute-start.1 = (bf16[2,512,128]{2,1,0:T(8,128)(2,1)S(1)}, bf16[2,512,128]{2,1,0:T(8,128)(2,1)S(1)}, u32[]{:S(2)}, u32[]{:S(2)}) collective-permute-start(bf16[2,512,128]{2,1,0:T(8,128)(2,1)S(1)} %copy-done), channel_id=1, source_target_pairs={{0,16},{8,24},{16,32},{24,40},{32,48},{40,56},{48,64},{56,72},{64,... | collective-permute-start | bytes 786440 | tf_op jit(solution)/shard_map/ppermute | solution.py:19
  48.7 6.6 %collective-permute-start = (bf16[2,512,128]{2,1,0:T(8,128)(2,1)S(1)}, bf16[2,512,128]{2,1,0:T(8,128)(2,1)S(1)}, u32[]{:S(2)}, u32[]{:S(2)}) collective-permute-start(bf16[2,512,128]{2,1,0:T(8,128)(2,1)S(1)} %copy-done), channel_id=1, source_target_pairs={{0,24},{8,32},{16,40},{24,48},{32,56},{40,64},{48,72},{56,80},{64,... | collective-permute-start | bytes 786440 | tf_op jit(solution)/shard_map/ppermute | solution.py:19
  55.3 2.7 collective-permute-start.2
  59.6 17.2 %collective-permute-done = bf16[2,512,128]{2,1,0:T(8,128)(2,1)S(1)} collective-permute-done((bf16[2,512,128]{2,1,0:T(8,128)(2,1)S(1)}, bf16[2,512,128]{2,1,0:T(8,128)(2,1)S(1)}, u32[]{:S(2)}, u32[]{:S(2)}) %collective-permute-start) | collective-permute-done | bytes 262176 | tf_op jit(solution)/shard_map/ppermute | solution.py:19
  76.8 16.0 %collective-permute-done.2 = bf16[2,512,128]{2,1,0:T(8,128)(2,1)S(1)} collective-permute-done((bf16[2,512,128]{2,1,0:T(8,128)(2,1)S(1)}, bf16[2,512,128]{2,1,0:T(8,128)(2,1)S(1)}, u32[]{:S(2)}, u32[]{:S(2)}) %collective-permute-start.2) | collective-permute-done | bytes 262176 | tf_op jit(solution)/shard_map/ppermute | solution.py:19
  92.9 138.4 %all-reduce.3.cloned.1.call-done = bf16[2,4,2048,128]{3,2,1,0:T(8,128)(2,1)} async-done(((bf16[2,4,2048,128]{3,2,1,0:T(8,128)(2,1)}), bf16[2,4,2048,128]{3,2,1,0:T(8,128)(2,1)}) %all-reduce.3.cloned.1.call-update) | async-done | bytes 4194320 | tf_op jit(solution)/shard_map/psum | solution.py:67
  231.3 144.0 %while.13 = (s32[]{:T(128)}, bf16[4,512,128]{1,2,0:T(8,128)(2,1)S(1)}, s32[4]{0:T(128)S(1)}, pred[4,2048]{1,0:T(4,128)(4,1)S(1)}, bf16[512,4,128]{0,2,1:T(8,128)...) while((s32[]{:T(128)}, ...), condition=%wide.region_7.9_spmd.clone.clone, body=%wide.region_1.8_spmd.clone.clone.sunk | while | flops 1168381440 | bytes 37260996 | solution.py:129
  240.3 2.5 fusion.80
  244.5 6.8 %select_reduce_fusion.4 = (f32[512]{0:T(512)S(1)}, f32[512,2048]{1,0:T(8,128)S(1)}) fusion(pred[2048]{0:T(1024)(128)(4,1)S(1)} %fusion.76, pred[2048]{0:T(1024)(128)(4,1)S(1)} %not.10, s32[]{:T(128)S(6)} %add.504, s32[]{:T(128)} %bitcast.118, s32[]{:T(128)S(6)} %add.505, s32[]{:T(128)} %bitcast.120, s32[]{:T(128)S(6)} %add.506, s32[]{:T(128)} %bitcast.122, ...), kind=kOutput, calls=%fused_computation.22.clone.1 | convolution fusion | flops 292552192 | bytes 4866084 | tf_op jit(solution)/shard_map/while/body/eval_jaxpr/dot_general | solution.py:111
  251.2 7.7 %fusion.81 = (f32[512]{0:T(512)S(1)}, f32[512]{0:T(512)S(1)}) fusion(f32[512,2048]{1,0:T(8,128)S(1)} %get-tuple-element.413, f32[512]{0:T(512)S(1)} %max.19, pred[2048]{0:T(1024)(128)(4,1)S(1)} %fusion.76, pred[2048]{0:T(1024)(128)(4,1)S(1)} %not.10, s32[]{:T(128)S(6)} %add.504, s32[]{:T(128)} %bitcast.118, s32[]{:T(128)S(6)} %add.505, s32[]{:T(128)} %bitcast.120, ...), kind=kLoop, calls=%fused_computation.36.clone.1 | loop fusion | flops 31456256 | bytes 8421408 | tf_op jit(solution)/shard_map/while/body/eval_jaxpr/reduce_sum | solution.py:120
  259.0 6.4 %fusion.82 = f32[512,128]{1,0:T(8,128)S(1)} fusion(f32[512,2048]{1,0:T(8,128)S(1)} %get-tuple-element.413, f32[512]{0:T(512)S(1)} %add.509, f32[512]{0:T(512)S(1)} %max.19, bf16[2,2048,1,128]{3,1,2,0:T(8,128)(2,1)S(1)} %get-tuple-element.469, s32[2048]{0:T(1024)S(1)} %get-tuple-element.472, s32[512]{0:T(512)S(1)} %get-tuple-element.473, ...), kind=kOutput, calls=%fused_computation.38.clone.1 | convolution fusion | flops 294649856 | bytes 4999200 | tf_op jit(solution)/shard_map/while/body/eval_jaxpr/dot_general | solution.py:126
  265.4 1.8 fusion.83
  276.3 2.5 fusion.80
  280.5 6.8 %select_reduce_fusion.4 = (f32[512]{0:T(512)S(1)}, f32[512,2048]{1,0:T(8,128)S(1)}) fusion(pred[2048]{0:T(1024)(128)(4,1)S(1)} %fusion.76, pred[2048]{0:T(1024)(128)(4,1)S(1)} %not.10, s32[]{:T(128)S(6)} %add.504, s32[]{:T(128)} %bitcast.118, s32[]{:T(128)S(6)} %add.505, s32[]{:T(128)} %bitcast.120, s32[]{:T(128)S(6)} %add.506, s32[]{:T(128)} %bitcast.122, ...), kind=kOutput, calls=%fused_computation.22.clone.1 | convolution fusion | flops 292552192 | bytes 4866084 | tf_op jit(solution)/shard_map/while/body/eval_jaxpr/dot_general | solution.py:111
  287.2 7.7 %fusion.81 = (f32[512]{0:T(512)S(1)}, f32[512]{0:T(512)S(1)}) fusion(f32[512,2048]{1,0:T(8,128)S(1)} %get-tuple-element.413, f32[512]{0:T(512)S(1)} %max.19, pred[2048]{0:T(1024)(128)(4,1)S(1)} %fusion.76, pred[2048]{0:T(1024)(128)(4,1)S(1)} %not.10, s32[]{:T(128)S(6)} %add.504, s32[]{:T(128)} %bitcast.118, s32[]{:T(128)S(6)} %add.505, s32[]{:T(128)} %bitcast.120, ...), kind=kLoop, calls=%fused_computation.36.clone.1 | loop fusion | flops 31456256 | bytes 8421408 | tf_op jit(solution)/shard_map/while/body/eval_jaxpr/reduce_sum | solution.py:120
  295.0 6.4 %fusion.82 = f32[512,128]{1,0:T(8,128)S(1)} fusion(f32[512,2048]{1,0:T(8,128)S(1)} %get-tuple-element.413, f32[512]{0:T(512)S(1)} %add.509, f32[512]{0:T(512)S(1)} %max.19, bf16[2,2048,1,128]{3,1,2,0:T(8,128)(2,1)S(1)} %get-tuple-element.469, s32[2048]{0:T(1024)S(1)} %get-tuple-element.472, s32[512]{0:T(512)S(1)} %get-tuple-element.473, ...), kind=kOutput, calls=%fused_computation.38.clone.1 | convolution fusion | flops 294649856 | bytes 4999200 | tf_op jit(solution)/shard_map/while/body/eval_jaxpr/dot_general | solution.py:126
  301.4 1.8 fusion.83
  312.3 2.5 fusion.80
  316.5 6.8 %select_reduce_fusion.4 = (f32[512]{0:T(512)S(1)}, f32[512,2048]{1,0:T(8,128)S(1)}) fusion(pred[2048]{0:T(1024)(128)(4,1)S(1)} %fusion.76, pred[2048]{0:T(1024)(128)(4,1)S(1)} %not.10, s32[]{:T(128)S(6)} %add.504, s32[]{:T(128)} %bitcast.118, s32[]{:T(128)S(6)} %add.505, s32[]{:T(128)} %bitcast.120, s32[]{:T(128)S(6)} %add.506, s32[]{:T(128)} %bitcast.122, ...), kind=kOutput, calls=%fused_computation.22.clone.1 | convolution fusion | flops 292552192 | bytes 4866084 | tf_op jit(solution)/shard_map/while/body/eval_jaxpr/dot_general | solution.py:111
  323.2 7.7 %fusion.81 = (f32[512]{0:T(512)S(1)}, f32[512]{0:T(512)S(1)}) fusion(f32[512,2048]{1,0:T(8,128)S(1)} %get-tuple-element.413, f32[512]{0:T(512)S(1)} %max.19, pred[2048]{0:T(1024)(128)(4,1)S(1)} %fusion.76, pred[2048]{0:T(1024)(128)(4,1)S(1)} %not.10, s32[]{:T(128)S(6)} %add.504, s32[]{:T(128)} %bitcast.118, s32[]{:T(128)S(6)} %add.505, s32[]{:T(128)} %bitcast.120, ...), kind=kLoop, calls=%fused_computation.36.clone.1 | loop fusion | flops 31456256 | bytes 8421408 | tf_op jit(solution)/shard_map/while/body/eval_jaxpr/reduce_sum | solution.py:120
  331.0 6.4 %fusion.82 = f32[512,128]{1,0:T(8,128)S(1)} fusion(f32[512,2048]{1,0:T(8,128)S(1)} %get-tuple-element.413, f32[512]{0:T(512)S(1)} %add.509, f32[512]{0:T(512)S(1)} %max.19, bf16[2,2048,1,128]{3,1,2,0:T(8,128)(2,1)S(1)} %get-tuple-element.469, s32[2048]{0:T(1024)S(1)} %get-tuple-element.472, s32[512]{0:T(512)S(1)} %get-tuple-element.473, ...), kind=kOutput, calls=%fused_computation.38.clone.1 | convolution fusion | flops 294649856 | bytes 4999200 | tf_op jit(solution)/shard_map/while/body/eval_jaxpr/dot_general | solution.py:126
  348.3 2.5 fusion.80
  352.5 6.8 %select_reduce_fusion.4 = (f32[512]{0:T(512)S(1)}, f32[512,2048]{1,0:T(8,128)S(1)}) fusion(pred[2048]{0:T(1024)(128)(4,1)S(1)} %fusion.76, pred[2048]{0:T(1024)(128)(4,1)S(1)} %not.10, s32[]{:T(128)S(6)} %add.504, s32[]{:T(128)} %bitcast.118, s32[]{:T(128)S(6)} %add.505, s32[]{:T(128)} %bitcast.120, s32[]{:T(128)S(6)} %add.506, s32[]{:T(128)} %bitcast.122, ...), kind=kOutput, calls=%fused_computation.22.clone.1 | convolution fusion | flops 292552192 | bytes 4866084 | tf_op jit(solution)/shard_map/while/body/eval_jaxpr/dot_general | solution.py:111
  359.2 7.7 %fusion.81 = (f32[512]{0:T(512)S(1)}, f32[512]{0:T(512)S(1)}) fusion(f32[512,2048]{1,0:T(8,128)S(1)} %get-tuple-element.413, f32[512]{0:T(512)S(1)} %max.19, pred[2048]{0:T(1024)(128)(4,1)S(1)} %fusion.76, pred[2048]{0:T(1024)(128)(4,1)S(1)} %not.10, s32[]{:T(128)S(6)} %add.504, s32[]{:T(128)} %bitcast.118, s32[]{:T(128)S(6)} %add.505, s32[]{:T(128)} %bitcast.120, ...), kind=kLoop, calls=%fused_computation.36.clone.1 | loop fusion | flops 31456256 | bytes 8421408 | tf_op jit(solution)/shard_map/while/body/eval_jaxpr/reduce_sum | solution.py:120
  367.0 6.4 %fusion.82 = f32[512,128]{1,0:T(8,128)S(1)} fusion(f32[512,2048]{1,0:T(8,128)S(1)} %get-tuple-element.413, f32[512]{0:T(512)S(1)} %add.509, f32[512]{0:T(512)S(1)} %max.19, bf16[2,2048,1,128]{3,1,2,0:T(8,128)(2,1)S(1)} %get-tuple-element.469, s32[2048]{0:T(1024)S(1)} %get-tuple-element.472, s32[512]{0:T(512)S(1)} %get-tuple-element.473, ...), kind=kOutput, calls=%fused_computation.38.clone.1 | convolution fusion | flops 294649856 | bytes 4999200 | tf_op jit(solution)/shard_map/while/body/eval_jaxpr/dot_general | solution.py:126
  375.3 6.5 %convolution_convert_fusion = bf16[512,4096]{1,0:T(8,128)(2,1)} fusion(bf16[512,512]{0,1:T(8,128)(2,1)S(1)} %bitcast.133, bf16[512,4096]{1,0:T(8,128)(2,1)} %param.19), kind=kOutput, calls=%fused_computation.82 | convolution fusion | flops 2149580800 | bytes 8912896 | tf_op jit(solution)/shard_map/dot_general | solution.py:131
  381.8 37.5 %reduce-scatter.2.cloned.1.call-done = bf16[512,512]{1,0:T(8,128)(2,1)} async-done(((bf16[512,4096]{1,0:T(8,128)(2,1)}), bf16[512,512]{1,0:T(8,128)(2,1)}) %reduce-scatter.2.cloned.1.call-update) | async-done | bytes 524304 | tf_op jit(solution)/shard_map/reduce_scatter | solution.py:132
  (117 shorter events, 24.8 us)
Async XLA Ops:
  6.5 224.8 %all-reduce.3.cloned.1.call-start = ((), (), s32[]{:S(2)}) async-start(), calls=%async_computation.1 | async-start | bytes 8388608 | tf_op jit(solution)/shard_map/psum | solution.py:67
  38.7 4.2 copy-start
  38.7 19.2 %copy-start.2 = (s32[32,4]{0,1:T(4,128)S(1)}, s32[32,4]{0,1:T(4,128)}, u32[]{:S(2)}) copy-start(s32[32,4]{0,1:T(4,128)} %param.17) | copy-start | bytes 1540
  38.8 19.3 %copy-start.3 = (s32[32,4]{0,1:T(4,128)S(1)}, s32[32,4]{0,1:T(4,128)}, u32[]{:S(2)}) copy-start(s32[32,4]{0,1:T(4,128)} %param.18) | copy-start | bytes 1540
  38.8 20.5 %copy-start.1 = (bf16[512,512]{1,0:T(8,128)(2,1)S(1)}, bf16[512,512]{1,0:T(8,128)(2,1)}, u32[]{:S(2)}) copy-start(bf16[512,512]{1,0:T(8,128)(2,1)} %param.12) | copy-start | bytes 1572868
  42.9 376.5 %reduce-scatter.2.cloned.1.call-start = ((), (), s32[]{:S(2)}) async-start(), calls=%async_computation.2 | async-start | bytes 4718592 | tf_op jit(solution)/shard_map/reduce_scatter | solution.py:132
  42.9 16.7 %collective-permute-start.1 = (bf16[2,512,128]{2,1,0:T(8,128)(2,1)S(1)}, bf16[2,512,128]{2,1,0:T(8,128)(2,1)S(1)}, u32[]{:S(2)}, u32[]{:S(2)}) collective-permute-start(bf16[2,512,128]{2,1,0:T(8,128)(2,1)S(1)} %copy-done), channel_id=1, source_target_pairs={{0,16},{8,24},{16,32},{24,40},{32,48},{40,56},{48,64},{56,72},{64,... | collective-permute-start | bytes 786440 | tf_op jit(solution)/shard_map/ppermute | solution.py:19
  48.7 28.1 %collective-permute-start = (bf16[2,512,128]{2,1,0:T(8,128)(2,1)S(1)}, bf16[2,512,128]{2,1,0:T(8,128)(2,1)S(1)}, u32[]{:S(2)}, u32[]{:S(2)}) collective-permute-start(bf16[2,512,128]{2,1,0:T(8,128)(2,1)S(1)} %copy-done), channel_id=1, source_target_pairs={{0,24},{8,32},{16,40},{24,48},{32,56},{40,64},{48,72},{56,80},{64,... | collective-permute-start | bytes 786440 | tf_op jit(solution)/shard_map/ppermute | solution.py:19
  55.3 37.6 %collective-permute-start.2 = (bf16[2,512,128]{2,1,0:T(8,128)(2,1)S(1)}, bf16[2,512,128]{2,1,0:T(8,128)(2,1)S(1)}, u32[]{:S(2)}, u32[]{:S(2)}) collective-permute-start(bf16[2,512,128]{2,1,0:T(8,128)(2,1)S(1)} %copy-done), channel_id=1, source_target_pairs={{0,8},{8,16},{16,24},{24,32},{32,40},{40,48},{48,56},{56,64},{64,7... | collective-permute-start | bytes 786440 | tf_op jit(solution)/shard_map/ppermute | solution.py:19
Sparse Core Ops, SparseCore 0:
  43.0 188.2 all-reduce.2
  381.9 37.3 reduce-scatter.1
where the time goes:
time: 429 us; the launch traced here: 426 us
  waiting for transfers between devices  209 us (49%)
  matrix products  72.5 us (17%)
  other arithmetic  55.2 us (13%)
  local copies, waits for them, and re-layouts  33.1 us (8%)
  loops' own time  27.5 us (6%)
  starting transfers between devices  15 us (3%)
  between operations  13.6 us (3%)
    psum x1, waiting for transfers between devices, local(): lax.psum(per_head_kv, 'ctx').astype(jnp.float32).astype(jnp.bfloat16)  138 us
    reduce_scatter x1, waiting for transfers between devices, local(): lax.psum_scatter(projected.astype(jnp.bfloat16), 'tp', scatter_dimension=...  37.5 us
    ppermute x3, waiting for transfers between devices, passed_along(): return lax.ppermute(block, axis, route)  33.2 us
    reduce_sum x4, other arithmetic, attend_head(): jnp.sum(band_exp, axis=1, keepdims=True)  30.9 us
    another operation x1, loops' own time, local(): attended = lax.map(attend_head, jnp.arange(local_heads, dtype=jnp.int32))  27.5 us
    dot_general x4, matrix products, attend_head(): lax.dot_general(query_rows, band_keys, contract, preferred_element_type=j...  27.1 us
    dot_general x4, matrix products, attend_head(): jnp.dot(band_probs, band_values, preferred_element_type=jnp.float32)  25.7 us
    ppermute x3, starting transfers between devices, passed_along(): return lax.ppermute(block, axis, route)  15 us
  transfers between devices with their start and end apart: 5, of which 4 were waited for; matrix products, arithmetic and copies ran while one was open for 0% of the time, Pallas kernels for 0%

commit v1 on v0

v1 whole, which is shorter than its diff:
```python
import functools
import math

import jax
import jax.numpy as jnp
from jax import lax
from jax.experimental import pallas as pl
from jax.experimental.pallas import tpu as pltpu
from jax.sharding import PartitionSpec as P

QH = 32
KVH = 8
HD = 128
BLK = 128
NG = 16
NS = 4
TOK = 512
PREFIX_BLOCKS = 512
WINDOW_TILES = 13
TILES = NG + WINDOW_TILES
CHUNKS = TOK // BLK
HEADS = QH // KVH
OFF = -1e30
EXP_SCALE = math.log2(math.e) / math.sqrt(HD)
OPEN, SHUT, CAUSAL, FIRST_BAND = 0, 1, 2, 3
BIAS_TILES = FIRST_BAND + HEADS * WINDOW_TILES


def pick_kernel(prefix_blocks, fresh_blocks, blocks_ref, prefix_ref, fresh_ref, out_ref):
    ctx = lax.axis_index("ctx")
    group = lax.axis_index("tp")
    for slot in range(NG):
        block = blocks_ref[group, slot]
        at_prefix = block - ctx * prefix_blocks
        at_fresh = block - PREFIX_BLOCKS - ctx * fresh_blocks
        in_prefix = (at_prefix >= 0) & (at_prefix < prefix_blocks) & (block < PREFIX_BLOCKS)
        in_fresh = (at_fresh >= 0) & (at_fresh < fresh_blocks)
        row_prefix = pl.multiple_of(jnp.clip(at_prefix, 0, prefix_blocks - 1) * BLK, BLK)
        row_fresh = pl.multiple_of(jnp.clip(at_fresh, 0, fresh_blocks - 1) * BLK, BLK)
        for part in range(2):
            from_prefix = prefix_ref[part, pl.ds(row_prefix, BLK), :]
            from_fresh = fresh_ref[part, pl.ds(row_fresh, BLK), :]
            zero = jnp.zeros_like(from_prefix)
            value = jnp.where(in_prefix, from_prefix, jnp.where(in_fresh, from_fresh, zero))
            out_ref[part, slot * BLK : (slot + 1) * BLK, :] = value


def make_bias(starts_ref, widths_ref, first_head, bias_ref):
    rows = lax.broadcasted_iota(jnp.int32, (BLK, BLK), 0)
    cols = lax.broadcasted_iota(jnp.int32, (BLK, BLK), 1)
    bias_ref[OPEN] = jnp.zeros((BLK, BLK), jnp.float32)
    bias_ref[SHUT] = jnp.full((BLK, BLK), OFF, jnp.float32)
    bias_ref[CAUSAL] = jnp.where(rows >= cols, 0.0, OFF)

    @pl.loop(0, HEADS)
    def per_head(head):
        @pl.loop(0, WINDOW_TILES)
        def per_tile(tile):
            distance = (rows - cols) + tile * BLK
            inside = jnp.zeros((BLK, BLK), jnp.bool_)
            for band in range(NS):
                start = starts_ref[first_head + head, band]
                width = widths_ref[first_head + head, band]
                inside = inside | ((distance >= start) & (distance < start + width))
            bias_ref[FIRST_BAND + head * WINDOW_TILES + tile] = jnp.where(inside, 0.0, OFF)


def attend_kernel(
    idx_ref, starts_ref, widths_ref, q_ref, vert_ref, win_ref, out_ref, bias_ref, s_ref, q_s, m_s, l_s, acc_s
):
    make_bias(starts_ref, widths_ref, lax.axis_index("tp") * HEADS, bias_ref)
    contract = (((1,), (1,)), ((), ()))

    @pl.loop(0, CHUNKS)
    def per_chunk(chunk):
        row0 = pl.multiple_of(chunk * BLK, BLK)
        for head in range(HEADS):
            q_s[head * BLK : (head + 1) * BLK, :] = q_ref[pl.ds(row0, BLK), head * HD : (head + 1) * HD]
        m_s[...] = jnp.full_like(m_s, OFF)

        def score(keys, tile, column, count):
            s = lax.dot_general(q_s[...], keys, contract, preferred_element_type=jnp.float32)
            for head in range(HEADS):
                rows = slice(head * BLK, (head + 1) * BLK)
                best = m_s[rows, :]
                for part in range(count):
                    piece = s[rows, part * BLK : (part + 1) * BLK]
                    piece = piece + bias_ref[idx_ref[chunk, head, tile + part]]
                    s_ref[rows, pl.ds(pl.multiple_of(column + part * BLK, BLK), BLK)] = piece
                    best = jnp.maximum(best, piece)
                m_s[rows, :] = best

        @pl.loop(0, NG // 2)
        def vertical(step):
            at = pl.multiple_of(step * 2 * BLK, 2 * BLK)
            score(vert_ref[0, pl.ds(at, 2 * BLK), :], step * 2, at, 2)

        @pl.loop(0, WINDOW_TILES // 2)
        def window(step):
            at = pl.multiple_of(step * 2 * BLK, 2 * BLK)
            score(win_ref[0, pl.ds(row0 + at, 2 * BLK), :], NG + step * 2, NG * BLK + at, 2)

        last = (WINDOW_TILES - 1) * BLK
        score(win_ref[0, pl.ds(row0 + last, BLK), :], TILES - 1, NG * BLK + last, 1)

        m_s[...] = jnp.broadcast_to(jnp.max(m_s[...], axis=1, keepdims=True), m_s.shape)
        l_s[...] = jnp.zeros_like(l_s)
        acc_s[...] = jnp.zeros_like(acc_s)

        def weigh(values, column, count):
            top = m_s[...]
            total = l_s[...]
            probs = []
            for part in range(count):
                piece = s_ref[:, pl.ds(pl.multiple_of(column + part * BLK, BLK), BLK)]
                piece = jnp.exp2((piece - top) * EXP_SCALE)
                total = total + piece
                probs.append(piece.astype(jnp.bfloat16))
            l_s[...] = total
            p = probs[0] if count == 1 else jnp.concatenate(probs, axis=1)
            acc_s[...] += jnp.dot(p, values, preferred_element_type=jnp.float32)

        @pl.loop(0, NG // 2)
        def vertical_values(step):
            at = pl.multiple_of(step * 2 * BLK, 2 * BLK)
            weigh(vert_ref[1, pl.ds(at, 2 * BLK), :], at, 2)

        @pl.loop(0, WINDOW_TILES // 2)
        def window_values(step):
            at = pl.multiple_of(step * 2 * BLK, 2 * BLK)
            weigh(win_ref[1, pl.ds(row0 + at, 2 * BLK), :], NG * BLK + at, 2)

        weigh(win_ref[1, pl.ds(row0 + last, BLK), :], NG * BLK + last, 1)
        result = acc_s[...] / jnp.sum(l_s[...], axis=1, keepdims=True)
        for head in range(HEADS):
            out_ref[pl.ds(row0, BLK), head * HD : (head + 1) * HD] = result[
                head * BLK : (head + 1) * BLK, :
            ].astype(jnp.bfloat16)


def bias_index(group_blocks, head_pick, ctx, tp):
    blocks = lax.dynamic_index_in_dim(group_blocks, tp, 0, keepdims=False)
    picks = lax.dynamic_slice_in_dim(head_pick, tp * HEADS, HEADS, 0) == 1
    chunk = jnp.arange(CHUNKS, dtype=jnp.int32)[:, None, None]
    own = PREFIX_BLOCKS + ctx * CHUNKS + chunk
    listed = blocks[None, None, :]
    vertical = jnp.where(listed < own, OPEN, jnp.where(listed == own, CAUSAL, SHUT))
    vertical = jnp.where(picks[None], vertical, SHUT)
    tile = jnp.arange(WINDOW_TILES, dtype=jnp.int32)[None, None, :]
    block = own + tile - (WINDOW_TILES - 1)
    seen = jnp.any((block[..., None] == blocks) & picks[None, :, None, :], axis=-1)
    head = jnp.arange(HEADS, dtype=jnp.int32)[None, :, None]
    band = FIRST_BAND + head * WINDOW_TILES + (WINDOW_TILES - 1 - tile)
    window = jnp.where(seen | (block < PREFIX_BLOCKS), SHUT, band)
    return jnp.concatenate([vertical, window], axis=-1).astype(jnp.int32)


def passed_along(block, axis, distance):
    devices = range(lax.axis_size(axis))
    route = [(i - distance, i) for i in devices if i - distance in devices]
    return lax.ppermute(block, axis, route)


VMEM = pl.BlockSpec(memory_space=pltpu.VMEM)
SMEM = pl.BlockSpec(memory_space=pltpu.SMEM)


def local(queries, prefix_kv, fresh_kv, group_blocks, head_pick, band_start, band_width, o_weight):
    ctx = lax.axis_index("ctx")
    tp = lax.axis_index("tp")
    picked = pl.pallas_call(
        functools.partial(pick_kernel, prefix_kv.shape[1] // BLK, fresh_kv.shape[1] // BLK),
        out_shape=jax.ShapeDtypeStruct((2, NG * BLK, HD), jnp.bfloat16),
        in_specs=[SMEM, VMEM, VMEM],
        out_specs=VMEM,
        compiler_params=pltpu.CompilerParams(vmem_limit_bytes=16 * 2**20),
    )(group_blocks, prefix_kv, fresh_kv)
    vert = lax.psum(picked, "ctx")
    earlier = [passed_along(fresh_kv, "ctx", back) for back in (3, 2, 1)]
    window = jnp.concatenate(earlier + [fresh_kv], axis=1)
    index = bias_index(group_blocks, head_pick, ctx, tp)
    rows = HEADS * BLK
    attended = pl.pallas_call(
        attend_kernel,
        out_shape=jax.ShapeDtypeStruct((TOK, HEADS * HD), jnp.bfloat16),
        in_specs=[SMEM, SMEM, SMEM, VMEM, VMEM, VMEM],
        out_specs=VMEM,
        scratch_shapes=[
            pltpu.VMEM((BIAS_TILES, BLK, BLK), jnp.float32),
            pltpu.VMEM((rows, TILES * BLK), jnp.float32),
            pltpu.VMEM((rows, HD), jnp.bfloat16),
            pltpu.VMEM((rows, BLK), jnp.float32),
            pltpu.VMEM((rows, BLK), jnp.float32),
            pltpu.VMEM((rows, HD), jnp.float32),
        ],
        compiler_params=pltpu.CompilerParams(vmem_limit_bytes=32 * 2**20),
    )(index, band_start, band_width, queries, vert, window)
    projected = jnp.dot(attended, o_weight, preferred_element_type=jnp.float32)
    return lax.psum_scatter(projected.astype(jnp.bfloat16), "tp", scatter_dimension=1, tiled=True)


def solution(mesh):
    return jax.shard_map(
        local,
        mesh=mesh,
        in_specs=(
            P("ctx", "tp"),
            P(None, "ctx", "tp"),
            P(None, "ctx", "tp"),
            P(),
            P(),
            P(),
            P(),
            P("tp", None),
        ),
        out_specs=P("ctx", "tp"),
        check_vma=False,
    )
```

time: 429 us -> 268 us (0.62)
  matrix products: 72.5 us -> 6.47 us
  other arithmetic: 55.2 us -> 3.23 us
  Pallas kernels: 0 us -> 37.2 us
  loops' own time: 27.5 us -> 0 us
  local copies, waits for them, and re-layouts: 33.1 us -> 6.6 us
  waiting for transfers between devices: 209 us -> 183 us
    dot_general x17 -> x1, matrix products: 72.5 us -> 6.47 us  [local(): projected = jnp.dot(attended, o_weight, preferred_element_type=jnp.float32)]
    pallas_call x0 -> x2, Pallas kernels: none -> 37.2 us  [the longest x1 35.2 us: local(): pl.pallas_call(attend_kernel, out_shape=jax.ShapeDtypeStruct((TOK, HEADS...]
    reduce_sum x4 -> x0, other arithmetic: 30.9 us -> none  [attend_head(): jnp.sum(band_exp, axis=1, keepdims=True)]
    another operation x1 -> x0, loops' own time: 27.5 us -> none  [local(): attended = lax.map(attend_head, jnp.arange(local_heads, dtype=jnp.int32))]
    ppermute x3, waiting for transfers between devices: 33.2 us -> 17.1 us  [passed_along(): return lax.ppermute(block, axis, route)]
    slice x12 -> x0, local copies, waits for them, and re-layouts: 15.4 us -> none  [the longest x4 10.1 us: attend_head(): vert_kv[1]]
    psum x1, waiting for transfers between devices: 138 us -> 126 us  [local(): vert = lax.psum(picked, 'ctx')]
    reshape x1 -> x0, other arithmetic: 10.8 us -> none  [local(): jnp.concatenate([prefix_kv, fresh_kv], axis=1)]
  transfers between devices with their start and end apart: 5 -> 5, of which waited for: 4 -> 4; matrix products, arithmetic and copies ran while one was open for 0% -> 2% of each run, Pallas kernels for 0% -> 1%
where the time goes in v1:
time: 268 us; the launch traced here: 265 us
  waiting for transfers between devices  183 us (68%)
  Pallas kernels  37.2 us (14%)
  starting transfers between devices  15 us (6%)
  between operations  13.5 us (5%)
  local copies, waits for them, and re-layouts  6.6 us (2%)
  matrix products  6.47 us (2%)
  other arithmetic  3.23 us (1%)
    psum x1, waiting for transfers between devices, local(): vert = lax.psum(picked, 'ctx')  126 us
    reduce_scatter x1, waiting for transfers between devices, local(): lax.psum_scatter(projected.astype(jnp.bfloat16), 'tp', scatter_dimension=...  39.6 us
    pallas_call x1, Pallas kernels, local(): pl.pallas_call(attend_kernel, out_shape=jax.ShapeDtypeStruct((TOK, HEADS...  35.2 us
    ppermute x3, waiting for transfers between devices, passed_along(): return lax.ppermute(block, axis, route)  17.1 us
    ppermute x3, starting transfers between devices, passed_along(): return lax.ppermute(block, axis, route)  15 us
    dot_general x1, matrix products, local(): projected = jnp.dot(attended, o_weight, preferred_element_type=jnp.float32)  6.47 us
    unnamed x12, local copies, waits for them, and re-layouts  5.61 us
  transfers between devices with their start and end apart: 5, of which 4 were waited for; matrix products, arithmetic and copies ran while one was open for 2% of the time, Pallas kernels for 1%

profile of v1, /device:TPU:1, one launch (start us, length us, event | category | flops | bytes accessed | tf_op | source)
XLA Modules:
  0.0 265.1 jit_solution(387301229345937949)
XLA Ops:
  6.5 5.7 %collective-permute-start.1 = (bf16[2,512,128]{2,1,0:T(8,128)(2,1)}, bf16[2,512,128]{2,1,0:T(8,128)(2,1)S(1)}, u32[]{:S(2)}, u32[]{:S(2)}) collective-permute-start(bf16[2,512,128]{2,1,0:T(8,128)(2,1)} %fresh_ref.1), channel_id=1, source_target_pairs={{0,16},{8,24},{16,32},{24,40},{32,48},{40,56},{48,64},{56,72},{64,... | collective-permute-start | bytes 786440 | tf_op jit(solution)/shard_map/ppermute | solution.py:161
  12.3 6.6 %collective-permute-start = (bf16[2,512,128]{2,1,0:T(8,128)(2,1)}, bf16[2,512,128]{2,1,0:T(8,128)(2,1)S(1)}, u32[]{:S(2)}, u32[]{:S(2)}) collective-permute-start(bf16[2,512,128]{2,1,0:T(8,128)(2,1)} %fresh_ref.1), channel_id=1, source_target_pairs={{0,24},{8,32},{16,40},{24,48},{32,56},{40,64},{48,72},{56,80},{64,... | collective-permute-start | bytes 786440 | tf_op jit(solution)/shard_map/ppermute | solution.py:161
  18.9 2.7 %collective-permute-start.2 = (bf16[2,512,128]{2,1,0:T(8,128)(2,1)}, bf16[2,512,128]{2,1,0:T(8,128)(2,1)S(1)}, u32[]{:S(2)}, u32[]{:S(2)}) collective-permute-start(bf16[2,512,128]{2,1,0:T(8,128)(2,1)} %fresh_ref.1), channel_id=1, source_target_pairs={{0,8},{8,16},{16,24},{24,32},{32,40},{40,48},{48,56},{56,64},{64,7... | collective-permute-start | bytes 786440 | tf_op jit(solution)/shard_map/ppermute | solution.py:161
  21.5 1.2 copy-done.1
  22.7 0.9 copy-done.2
  23.7 0.7 copy-done.4
  24.4 2.0 shard_map.82
  26.4 0.0 all-reduce.2.cloned.1.call-update
  26.4 0.0 reduce-scatter.2.cloned.1.call-start
  26.5 0.1 broadcast_compare_fusion.1
  26.6 0.1 add_add_fusion
  26.6 0.7 dynamic-slice_bitcast_fusion
  27.3 0.8 dynamic-slice_compare_fusion
  28.1 0.1 copy.14
  28.2 0.1 select_select_fusion
  28.3 0.1 broadcast_compare_fusion
  28.3 1.0 and_reduce_fusion
  29.3 0.1 copy.17
  29.5 0.1 copy.15
  29.5 0.8 copy.18.starts_ref
  30.3 0.8 copy.19.widths_ref
  31.1 0.1 broadcast_add_fusion
  31.1 0.1 pad_add_fusion.idx_ref
  31.2 9.6 %collective-permute-done = bf16[2,512,128]{2,1,0:T(8,128)(2,1)S(1)} collective-permute-done((bf16[2,512,128]{2,1,0:T(8,128)(2,1)}, bf16[2,512,128]{2,1,0:T(8,128)(2,1)S(1)}, u32[]{:S(2)}, u32[]{:S(2)}) %collective-permute-start) | collective-permute-done | bytes 262176 | tf_op jit(solution)/shard_map/ppermute | solution.py:161
  40.8 7.5 %collective-permute-done.2 = bf16[2,512,128]{2,1,0:T(8,128)(2,1)S(1)} collective-permute-done((bf16[2,512,128]{2,1,0:T(8,128)(2,1)}, bf16[2,512,128]{2,1,0:T(8,128)(2,1)S(1)}, u32[]{:S(2)}, u32[]{:S(2)}) %collective-permute-start.2) | collective-permute-done | bytes 262176 | tf_op jit(solution)/shard_map/ppermute | solution.py:161
  48.3 1.0 pad_maximum_fusion.win_ref
  49.3 126.4 %all-reduce.2.cloned.1.call-done.vert_ref = bf16[2,2048,128]{2,1,0:T(8,128)(2,1)} async-done(((bf16[2,2048,128]{2,1,0:T(8,128)(2,1)}), bf16[2,2048,128]{2,1,0:T(8,128)(2,1)}) %all-reduce.2.cloned.1.call-update) | async-done | bytes 1048592 | tf_op jit(solution)/shard_map/psum | solution.py:178
  175.7 1.2 copy-done
  176.9 35.2 %shard_map.83 = bf16[512,512]{1,0:T(8,128)(2,1)S(1)} custom-call(s32[4,4,29]{2,1,0:T(4,128)S(1)} %pad_add_fusion.idx_ref, s32[32,4]{1,0:T(8,128)S(1)} %copy.18.starts_ref, s32[32,4]{1,0:T(8,128)S(1)} %copy.19.widths_ref, bf16[512,512]{1,0:T(8,128)(2,1)S(1)} %copy-done.3, bf16[2,2048,128]{2,1,0:T(8,128)(2,1)S(1)} %copy-done, ...), custom_call_target="tpu_custom_call" | custom-call | tf_op jit(solution)/shard_map/pallas_call | solution.py:183
  212.1 6.5 %convolution_convert_fusion = bf16[512,4096]{1,0:T(8,128)(2,1)} fusion(bf16[512,512]{1,0:T(8,128)(2,1)S(1)} %shard_map.83, bf16[512,4096]{1,0:T(8,128)(2,1)} %param.15), kind=kOutput, calls=%fused_computation | convolution fusion | flops 2149580800 | bytes 8912896 | tf_op jit(solution)/shard_map/dot_general | solution.py:198
  218.6 0.0 reduce-scatter.2.cloned.1.call-update
  218.6 39.6 %reduce-scatter.2.cloned.1.call-done = bf16[512,512]{1,0:T(8,128)(2,1)} async-done(((bf16[512,4096]{1,0:T(8,128)(2,1)}), bf16[512,512]{1,0:T(8,128)(2,1)}) %reduce-scatter.2.cloned.1.call-update) | async-done | bytes 524304 | tf_op jit(solution)/shard_map/reduce_scatter | solution.py:199
  (13 shorter events, 0.0 us)
Async XLA Ops:
  6.5 169.2 %all-reduce.2.cloned.1.call-start = ((), (), s32[]{:S(2)}) async-start(), calls=%async_computation.1 | async-start | bytes 2097152 | tf_op jit(solution)/shard_map/psum | solution.py:178
  6.5 24.7 %collective-permute-start.1 = (bf16[2,512,128]{2,1,0:T(8,128)(2,1)}, bf16[2,512,128]{2,1,0:T(8,128)(2,1)S(1)}, u32[]{:S(2)}, u32[]{:S(2)}) collective-permute-start(bf16[2,512,128]{2,1,0:T(8,128)(2,1)} %fresh_ref.1), channel_id=1, source_target_pairs={{0,16},{8,24},{16,32},{24,40},{32,48},{40,56},{48,64},{56,72},{64,... | collective-permute-start | bytes 786440 | tf_op jit(solution)/shard_map/ppermute | solution.py:161
  12.3 28.5 %collective-permute-start = (bf16[2,512,128]{2,1,0:T(8,128)(2,1)}, bf16[2,512,128]{2,1,0:T(8,128)(2,1)S(1)}, u32[]{:S(2)}, u32[]{:S(2)}) collective-permute-start(bf16[2,512,128]{2,1,0:T(8,128)(2,1)} %fresh_ref.1), channel_id=1, source_target_pairs={{0,24},{8,32},{16,40},{24,48},{32,56},{40,64},{48,72},{56,80},{64,... | collective-permute-start | bytes 786440 | tf_op jit(solution)/shard_map/ppermute | solution.py:161
  18.9 29.5 %collective-permute-start.2 = (bf16[2,512,128]{2,1,0:T(8,128)(2,1)}, bf16[2,512,128]{2,1,0:T(8,128)(2,1)S(1)}, u32[]{:S(2)}, u32[]{:S(2)}) collective-permute-start(bf16[2,512,128]{2,1,0:T(8,128)(2,1)} %fresh_ref.1), channel_id=1, source_target_pairs={{0,8},{8,16},{16,24},{24,32},{32,40},{40,48},{48,56},{56,64},{64,7... | collective-permute-start | bytes 786440 | tf_op jit(solution)/shard_map/ppermute | solution.py:161
  21.5 1.2 copy-start.1
  22.7 0.9 copy-start.2
  23.7 0.7 copy-start.4
  24.4 151.3 %copy-start.3 = (bf16[512,512]{1,0:T(8,128)(2,1)S(1)}, bf16[512,512]{1,0:T(8,128)(2,1)}, u32[]{:S(2)}) copy-start(bf16[512,512]{1,0:T(8,128)(2,1)} %q_ref.1) | copy-start | bytes 1572868
  26.4 231.8 %reduce-scatter.2.cloned.1.call-start = ((), (), s32[]{:S(2)}) async-start(), calls=%async_computation.2 | async-start | bytes 4718592 | tf_op jit(solution)/shard_map/reduce_scatter | solution.py:199
  175.7 1.2 copy-start
Sparse Core Ops, SparseCore 0:
  26.5 149.1 all-reduce.1
  218.7 39.4 reduce-scatter.1

commit v2 on v1

--- a/solution.py
+++ b/solution.py
@@ -20,29 +20,18 @@
 TILES = NG + WINDOW_TILES
 CHUNKS = TOK // BLK
 HEADS = QH // KVH
+X_SIZE = 4
+Z_SIZE = 8
+QUARTER = NG * BLK // X_SIZE
+HALF = QUARTER // 2
+PIECE = QUARTER // Z_SIZE
+PREFIX_DEV = 16
+FRESH_DEV = 4
+MESH = pl.DeviceIdType.MESH
 OFF = -1e30
 EXP_SCALE = math.log2(math.e) / math.sqrt(HD)
 OPEN, SHUT, CAUSAL, FIRST_BAND = 0, 1, 2, 3
 BIAS_TILES = FIRST_BAND + HEADS * WINDOW_TILES
-
-
-def pick_kernel(prefix_blocks, fresh_blocks, blocks_ref, prefix_ref, fresh_ref, out_ref):
-    ctx = lax.axis_index("ctx")
-    group = lax.axis_index("tp")
-    for slot in range(NG):
-        block = blocks_ref[group, slot]
-        at_prefix = block - ctx * prefix_blocks
-        at_fresh = block - PREFIX_BLOCKS - ctx * fresh_blocks
-        in_prefix = (at_prefix >= 0) & (at_prefix < prefix_blocks) & (block < PREFIX_BLOCKS)
-        in_fresh = (at_fresh >= 0) & (at_fresh < fresh_blocks)
-        row_prefix = pl.multiple_of(jnp.clip(at_prefix, 0, prefix_blocks - 1) * BLK, BLK)
-        row_fresh = pl.multiple_of(jnp.clip(at_fresh, 0, fresh_blocks - 1) * BLK, BLK)
-        for part in range(2):
-            from_prefix = prefix_ref[part, pl.ds(row_prefix, BLK), :]
-            from_fresh = fresh_ref[part, pl.ds(row_fresh, BLK), :]
-            zero = jnp.zeros_like(from_prefix)
-            value = jnp.where(in_prefix, from_prefix, jnp.where(in_fresh, from_fresh, zero))
-            out_ref[part, slot * BLK : (slot + 1) * BLK, :] = value
 
 
 def make_bias(starts_ref, widths_ref, first_head, bias_ref):
@@ -65,10 +54,7 @@
             bias_ref[FIRST_BAND + head * WINDOW_TILES + tile] = jnp.where(inside, 0.0, OFF)
 
 
-def attend_kernel(
-    idx_ref, starts_ref, widths_ref, q_ref, vert_ref, win_ref, out_ref, bias_ref, s_ref, q_s, m_s, l_s, acc_s
-):
-    make_bias(starts_ref, widths_ref, lax.axis_index("tp") * HEADS, bias_ref)
+def attend(idx_ref, q_ref, vert_ref, win_ref, out_ref, bias_ref, s_ref, q_s, m_s, l_s, acc_s):
     contract = (((1,), (1,)), ((), ()))
 
     @pl.loop(0, CHUNKS)
@@ -155,48 +141,299 @@
     return jnp.concatenate([vertical, window], axis=-1).astype(jnp.int32)
 
 
-def passed_along(block, axis, distance):
-    devices = range(lax.axis_size(axis))
-    route = [(i - distance, i) for i in devices if i - distance in devices]
-    return lax.ppermute(block, axis, route)
+def pick(blocks_ref, prefix_ref, fresh_ref, out_ref, part):
+    ctx = lax.axis_index("ctx")
+    group = lax.axis_index("tp")
+    for slot in range(NG):
+        block = blocks_ref[group, slot]
+        at_prefix = block - ctx * PREFIX_DEV
+        at_fresh = block - PREFIX_BLOCKS - ctx * FRESH_DEV
+        in_prefix = (at_prefix >= 0) & (at_prefix < PREFIX_DEV) & (block < PREFIX_BLOCKS)
+        in_fresh = (at_fresh >= 0) & (at_fresh < FRESH_DEV)
+        from_prefix = prefix_ref[part, jnp.clip(at_prefix, 0, PREFIX_DEV - 1)]
+        from_fresh = fresh_ref[part, jnp.clip(at_fresh, 0, FRESH_DEV - 1)]
+        zero = jnp.zeros_like(from_prefix)
+        value = jnp.where(in_prefix, from_prefix, jnp.where(in_fresh, from_fresh, zero))
+        out_ref[part, slot * BLK : (slot + 1) * BLK, :] = value
+
+
+class Sends:
+    def __init__(self, send_sem, recv_sem):
+        self.send_sem, self.recv_sem, self.used, self.started = send_sem, recv_sem, 0, []
+
+    def make(self, src, dst, device):
+        slot = self.used
+        self.used += 1
+        return pltpu.make_async_remote_copy(
+            src_ref=src,
+            dst_ref=dst,
+            send_sem=self.send_sem.at[slot],
+            recv_sem=self.recv_sem.at[slot],
+            device_id=device,
+            device_id_type=MESH,
+        )
+
+    def start(self, src, dst, device):
+        copy = self.make(src, dst, device)
+        copy.start()
+        self.started.append(copy)
+        return copy
+
+    def finish(self):
+        for copy in self.started:
+            copy.wait_send()
+
+
+def collect(blocks_ref, prefix_ref, fresh_ref, vert_ref, win_ref, mine, far_in, near_in, piece_in, sends):
+    ctx = lax.axis_index("ctx")
+    tp = lax.axis_index("tp")
+    x, z = ctx // Z_SIZE, ctx % Z_SIZE
+    x_far, x_right, x_left = (x + 2) % X_SIZE, (x + 1) % X_SIZE, (x + 3) % X_SIZE
+    right = (x_right * Z_SIZE + z, tp)
+    left = (x_left * Z_SIZE + z, tp)
+    along = [(x * Z_SIZE + (z + k) % Z_SIZE, tp) for k in range(1, Z_SIZE)]
+    size = X_SIZE * Z_SIZE
+    after = ((ctx + 1) % size, tp)
+    before = ((ctx + size - 1) % size, tp)
+
+    barrier = pltpu.get_barrier_semaphore()
+    partners = [right, left] + along + [after, before]
+    for device in partners:
+        pl.semaphore_signal(barrier, inc=1, device_id=device, device_id_type=MESH)
+    for part in range(2):
+        pick(blocks_ref, prefix_ref, fresh_ref, mine, part)
+        for block in range(FRESH_DEV):
+            win_ref[part, 3 * TOK + block * BLK : 3 * TOK + (block + 1) * BLK, :] = fresh_ref[part, block]
+    pl.semaphore_wait(barrier, len(partners))
+
+    def rows(start, count):
+        return pl.ds(pl.multiple_of(start, PIECE), count)
+
+    def hand_on(part, age):
+        return sends.start(
+            win_ref.at[part, pl.ds((3 - age) * TOK, TOK), :],
+            win_ref.at[part, pl.ds((2 - age) * TOK, TOK), :],
+            after,
+        )
+
+    far, near, window = {}, {}, {}
+    for part in range(2):
+        far[part] = [
+            sends.start(mine.at[part, rows(x_far * QUARTER, HALF), :], far_in.at[part, 0], right),
+            sends.start(mine.at[part, rows(x_far * QUARTER + HALF, HALF), :], far_in.at[part, 1], left),
+        ]
+        near[part] = [
+            sends.start(
+                mine.at[part, rows(x_right * QUARTER + HALF, HALF), :], near_in.at[part, 0, pl.ds(HALF, HALF), :], right
+            ),
+            sends.start(mine.at[part, rows(x_left * QUARTER, HALF), :], near_in.at[part, 1, pl.ds(0, HALF), :], left),
+        ]
+        window[part, 0] = hand_on(part, 0)
+    for part in range(2):
+        far[part][0].wait_recv()
+        mine[part, rows(x_right * QUARTER, HALF), :] += far_in[part, 0]
+        near[part].append(
+            sends.start(mine.at[part, rows(x_right * QUARTER, HALF), :], near_in.at[part, 0, pl.ds(0, HALF), :], right)
+        )
+        far[part][1].wait_recv()
+        mine[part, rows(x_left * QUARTER + HALF, HALF), :] += far_in[part, 1]
+        near[part].append(
+            sends.start(
+                mine.at[part, rows(x_left * QUARTER + HALF, HALF), :], near_in.at[part, 1, pl.ds(HALF, HALF), :], left
+            )
+        )
+    pieces = {}
+    for part in range(2):
+        for copy in near[part]:
+            copy.wait_recv()
+        own = rows(x * QUARTER, QUARTER)
+        mine[part, own, :] = mine[part, own, :] + near_in[part, 0] + near_in[part, 1]
+        pieces[part] = [
+            sends.start(
+                mine.at[part, rows(x * QUARTER + (z + k) % Z_SIZE * PIECE, PIECE), :],
+                piece_in.at[part, k - 1],
+                along[k - 1],
+            )
+            for k in range(1, Z_SIZE)
+        ]
+        window[part, 0].wait_recv()
+        window[part, 1] = hand_on(part, 1)
+    gathered = {}
+    for part in range(2):
+        at = rows(x * QUARTER + z * PIECE, PIECE)
+        total = mine[part, at, :]
+        for k in range(1, Z_SIZE):
+            pieces[part][k - 1].wait_recv()
+            total = total + piece_in[part, k - 1]
+        vert_ref[part, at, :] = total
+        gathered[part] = [
+            sends.start(vert_ref.at[part, at, :], vert_ref.at[part, at, :], along[k - 1]) for k in range(1, Z_SIZE)
+        ]
+        window[part, 1].wait_recv()
+        window[part, 2] = hand_on(part, 2)
+    spread = {}
+    for part in range(2):
+        for copy in gathered[part]:
+            copy.wait_recv()
+        spread[part] = []
+        for start in (0, HALF):
+            at = rows(x * QUARTER + start, HALF)
+            for device in (right, left):
+                spread[part].append(sends.start(vert_ref.at[part, at, :], vert_ref.at[part, at, :], device))
+    relayed = []
+    for part in range(2):
+        top_right, top_left, low_right, low_left = spread[part]
+        top_right.wait_recv()
+        at = rows(x_left * QUARTER, HALF)
+        relayed.append(sends.start(vert_ref.at[part, at, :], vert_ref.at[part, at, :], right))
+        low_left.wait_recv()
+        at = rows(x_right * QUARTER + HALF, HALF)
+        relayed.append(sends.start(vert_ref.at[part, at, :], vert_ref.at[part, at, :], left))
+        top_left.wait_recv()
+        low_right.wait_recv()
+    for copy in relayed:
+        copy.wait_recv()
+    for part in range(2):
+        window[part, 2].wait_recv()
+    sends.finish()
+
+
+def attend_kernel(
+    blocks_ref, idx_ref, starts_ref, widths_ref, q_ref, prefix_ref, fresh_ref, out_ref,
+    mine, far_in, near_in, piece_in, vert_ref, win_ref, send_sem, recv_sem,
+    bias_ref, s_ref, q_s, m_s, l_s, acc_s,
+):
+    sends = Sends(send_sem, recv_sem)
+    collect(blocks_ref, prefix_ref, fresh_ref, vert_ref, win_ref, mine, far_in, near_in, piece_in, sends)
+    make_bias(starts_ref, widths_ref, lax.axis_index("tp") * HEADS, bias_ref)
+    attend(idx_ref, q_ref, vert_ref, win_ref, out_ref, bias_ref, s_ref, q_s, m_s, l_s, acc_s)
 
 
 VMEM = pl.BlockSpec(memory_space=pltpu.VMEM)
 SMEM = pl.BlockSpec(memory_space=pltpu.SMEM)
+COPIES = 64
+
+
+def project_kernel(att_ref, w_ref, out_ref, w_in, att_in, mine, far_in, near_in, send_sem, recv_sem):
+    ctx = lax.axis_index("ctx")
+    tp = lax.axis_index("tp")
+    y, core = tp // 2, tp % 2
+    y_far, y_right, y_left = (y + 2) % 4, (y + 1) % 4, (y + 3) % 4
+    pair = (ctx, y * 2 + (1 - core))
+    right = (ctx, y_right * 2 + core)
+    left = (ctx, y_left * 2 + core)
+    barrier = pltpu.get_barrier_semaphore()
+    for device in (pair, right, left):
+        pl.semaphore_signal(barrier, inc=1, device_id=device, device_id_type=MESH)
+    pl.semaphore_wait(barrier, 3)
+    sends = Sends(send_sem, recv_sem)
+    att = sends.start(att_ref, att_in, pair)
+    weights = [
+        sends.start(w_ref.at[:, pl.ds(pl.multiple_of((to * 2 + 1 - core) * TOK, TOK), TOK)], w_in.at[to], pair)
+        for to in range(4)
+    ]
+    att.wait_recv()
+    for copy in weights:
+        copy.wait_recv()
+
+    def term(to, start, count):
+        columns = pl.ds(pl.multiple_of((to * 2 + core) * TOK, TOK), TOK)
+        at = slice(start, start + count)
+        total = jnp.dot(att_ref[at, :], w_ref[:, columns], preferred_element_type=jnp.float32)
+        return total + jnp.dot(att_in[at, :], w_in[to], preferred_element_type=jnp.float32)
+
+    half = TOK // 2
+    top, low = pl.ds(0, half), pl.ds(half, half)
+    mine[0, :half, :] = term(y_far, 0, half).astype(jnp.bfloat16)
+    far_top = sends.start(mine.at[0, top, :], far_in.at[0], right)
+    mine[0, half:, :] = term(y_far, half, half).astype(jnp.bfloat16)
+    far_low = sends.start(mine.at[0, low, :], far_in.at[1], left)
+    mine[1, half:, :] = term(y_right, half, half).astype(jnp.bfloat16)
+    right_low = sends.start(mine.at[1, low, :], near_in.at[0, low, :], right)
+    mine[2, :half, :] = term(y_left, 0, half).astype(jnp.bfloat16)
+    left_top = sends.start(mine.at[2, top, :], near_in.at[1, top, :], left)
+    near = term(y_right, 0, half)
+    far_top.wait_recv()
+    mine[1, :half, :] = (near + far_in[0].astype(jnp.float32)).astype(jnp.bfloat16)
+    right_top = sends.start(mine.at[1, top, :], near_in.at[0, top, :], right)
+    near = term(y_left, half, half)
+    far_low.wait_recv()
+    mine[2, half:, :] = (near + far_in[1].astype(jnp.float32)).astype(jnp.bfloat16)
+    left_low = sends.start(mine.at[2, low, :], near_in.at[1, low, :], left)
+    own_top = term(y, 0, half)
+    own_low = term(y, half, half)
+
+    def add(own, at):
+        from_left = near_in[0, at, :].astype(jnp.float32)
+        from_right = near_in[1, at, :].astype(jnp.float32)
+        out_ref[at, :] = (own + from_left + from_right).astype(jnp.bfloat16)
+
+    left_top.wait_recv()
+    right_top.wait_recv()
+    add(own_top, slice(0, half))
+    right_low.wait_recv()
+    left_low.wait_recv()
+    add(own_low, slice(half, TOK))
+    sends.finish()
 
 
 def local(queries, prefix_kv, fresh_kv, group_blocks, head_pick, band_start, band_width, o_weight):
     ctx = lax.axis_index("ctx")
     tp = lax.axis_index("tp")
-    picked = pl.pallas_call(
-        functools.partial(pick_kernel, prefix_kv.shape[1] // BLK, fresh_kv.shape[1] // BLK),
-        out_shape=jax.ShapeDtypeStruct((2, NG * BLK, HD), jnp.bfloat16),
-        in_specs=[SMEM, VMEM, VMEM],
-        out_specs=VMEM,
-        compiler_params=pltpu.CompilerParams(vmem_limit_bytes=16 * 2**20),
-    )(group_blocks, prefix_kv, fresh_kv)
-    vert = lax.psum(picked, "ctx")
-    earlier = [passed_along(fresh_kv, "ctx", back) for back in (3, 2, 1)]
-    window = jnp.concatenate(earlier + [fresh_kv], axis=1)
     index = bias_index(group_blocks, head_pick, ctx, tp)
     rows = HEADS * BLK
+    bf16 = jnp.bfloat16
     attended = pl.pallas_call(
         attend_kernel,
-        out_shape=jax.ShapeDtypeStruct((TOK, HEADS * HD), jnp.bfloat16),
-        in_specs=[SMEM, SMEM, SMEM, VMEM, VMEM, VMEM],
+        out_shape=jax.ShapeDtypeStruct((TOK, HEADS * HD), bf16),
+        in_specs=[SMEM, SMEM, SMEM, SMEM, VMEM, VMEM, VMEM],
         out_specs=VMEM,
         scratch_shapes=[
+            pltpu.VMEM((2, NG * BLK, HD), bf16),
+            pltpu.VMEM((2, 2, HALF, HD), bf16),
+            pltpu.VMEM((2, 2, QUARTER, HD), bf16),
+            pltpu.VMEM((2, Z_SIZE - 1, PIECE, HD), bf16),
+            pltpu.VMEM((2, NG * BLK, HD), bf16),
+            pltpu.VMEM((2, 4 * TOK, HD), bf16),
+            pltpu.SemaphoreType.DMA((COPIES,)),
+            pltpu.SemaphoreType.DMA((COPIES,)),
             pltpu.VMEM((BIAS_TILES, BLK, BLK), jnp.float32),
             pltpu.VMEM((rows, TILES * BLK), jnp.float32),
-            pltpu.VMEM((rows, HD), jnp.bfloat16),
+            pltpu.VMEM((rows, HD), bf16),
             pltpu.VMEM((rows, BLK), jnp.float32),
             pltpu.VMEM((rows, BLK), jnp.float32),
             pltpu.VMEM((rows, HD), jnp.float32),
         ],
-        compiler_params=pltpu.CompilerParams(vmem_limit_bytes=32 * 2**20),
-    )(index, band_start, band_width, queries, vert, window)
-    projected = jnp.dot(attended, o_weight, preferred_element_type=jnp.float32)
-    return lax.psum_scatter(projected.astype(jnp.bfloat16), "tp", scatter_dimension=1, tiled=True)
+        compiler_params=pltpu.CompilerParams(
+            vmem_limit_bytes=48 * 2**20, collective_id=0, has_side_effects=True
+        ),
+    )(
+        group_blocks,
+        index,
+        band_start,
+        band_width,
+        queries,
+        prefix_kv.reshape(2, PREFIX_DEV, BLK, HD),
+        fresh_kv.reshape(2, FRESH_DEV, BLK, HD),
+    )
+    return pl.pallas_call(
+        project_kernel,
+        out_shape=jax.ShapeDtypeStruct((TOK, TOK), bf16),
+        in_specs=[VMEM, VMEM],
+        out_specs=VMEM,
+        scratch_shapes=[
+            pltpu.VMEM((4, TOK, TOK), bf16),
+            pltpu.VMEM((TOK, TOK), bf16),
+            pltpu.VMEM((3, TOK, TOK), bf16),
+            pltpu.VMEM((2, TOK // 2, TOK), bf16),
+            pltpu.VMEM((2, TOK, TOK), bf16),
+            pltpu.SemaphoreType.DMA((16,)),
+            pltpu.SemaphoreType.DMA((16,)),
+        ],
+        compiler_params=pltpu.CompilerParams(
+            vmem_limit_bytes=48 * 2**20, collective_id=1, has_side_effects=True
+        ),
+    )(attended, o_weight)
 
 
 def solution(mesh):

time: 268 us -> 129 us (0.48)
  waiting for transfers between devices: 183 us -> 0 us
  Pallas kernels: 37.2 us -> 117 us
  starting transfers between devices: 15 us -> 0 us
  between operations: 13.5 us -> 0.04 us
  matrix products: 6.47 us -> 0 us
  local copies, waits for them, and re-layouts: 6.6 us -> 9.41 us
    psum x1 -> x0, waiting for transfers between devices: 126 us -> none  [local(): vert = lax.psum(picked, 'ctx')]
    pallas_call x1, Pallas kernels: 35.2 us -> 85.7 us  [local(): pl.pallas_call(attend_kernel, out_shape=jax.ShapeDtypeStruct((TOK, HEADS...]
    reduce_scatter x1 -> x0, waiting for transfers between devices: 39.6 us -> none  [local(): lax.psum_scatter(projected.astype(jnp.bfloat16), 'tp', scatter_dimension=...]
    pallas_call x1, Pallas kernels: 1.99 us -> 30.8 us  [local(): pl.pallas_call(project_kernel, out_shape=jax.ShapeDtypeStruct((TOK, TOK),...]
    ppermute x3 -> x0, waiting for transfers between devices: 17.1 us -> none  [passed_along(): return lax.ppermute(block, axis, route)]
    ppermute x3 -> x0, starting transfers between devices: 15 us -> none  [passed_along(): return lax.ppermute(block, axis, route)]
    dot_general x1 -> x0, matrix products: 6.47 us -> none  [local(): projected = jnp.dot(attended, o_weight, preferred_element_type=jnp.float32)]
    unnamed x12 -> x13, local copies, waits for them, and re-layouts: 5.61 us -> 8.41 us
  transfers between devices with their start and end apart: 5 -> 0, of which waited for: 4 -> 0; matrix products, arithmetic and copies ran while one was open for 2% -> 0% of each run, Pallas kernels for 1% -> 0%
where the time goes in v2:
time: 129 us; the launch traced here: 128 us
  Pallas kernels  117 us (91%)
  local copies, waits for them, and re-layouts  9.41 us (7%)
  other arithmetic  2.23 us (2%)
    pallas_call x1, Pallas kernels, local(): pl.pallas_call(attend_kernel, out_shape=jax.ShapeDtypeStruct((TOK, HEADS...  85.7 us
    pallas_call x1, Pallas kernels, local(): pl.pallas_call(project_kernel, out_shape=jax.ShapeDtypeStruct((TOK, TOK),...  30.8 us
    unnamed x13, local copies, waits for them, and re-layouts  8.41 us

profile of v2, /device:TPU:1, one launch (start us, length us, event | category | flops | bytes accessed | tf_op | source)
XLA Modules:
  0.0 128.3 jit_solution(11693443427649403937)
XLA Ops:
  0.0 0.7 dynamic-slice_bitcast_fusion
  0.7 0.1 broadcast_compare_fusion.1
  0.8 0.1 broadcast_add_fusion
  0.9 0.8 dynamic-slice_compare_fusion
  1.6 0.1 copy.14
  1.7 0.1 add_add_fusion
  1.8 0.1 broadcast_compare_fusion
  1.9 1.0 and_reduce_fusion
  2.9 0.1 copy.17
  3.0 0.1 select_select_fusion
  3.1 0.1 copy.15
  3.2 0.1 pad_add_fusion.idx_ref
  3.2 0.8 copy.18.starts_ref
  4.0 0.8 copy.19.widths_ref
  4.8 0.0 copy-start.1
  4.8 1.2 copy-done.1
  6.0 0.0 copy-start.2
  6.0 1.0 copy-done.2
  7.0 0.0 copy-start.3
  7.0 0.9 copy-done.3
  8.0 0.0 copy-start.4
  8.0 0.7 copy-done.4
  8.7 85.7 %shard_map.82.att_ref = bf16[512,512]{1,0:T(8,128)(2,1)S(1)} custom-call(s32[8,16]{1,0:T(8,128)S(1)} %copy-done.4, s32[4,4,29]{2,1,0:T(4,128)S(1)} %pad_add_fusion.idx_ref, s32[32,4]{1,0:T(8,128)S(1)} %copy.18.starts_ref, s32[32,4]{1,0:T(8,128)S(1)} %copy.19.widths_ref, bf16[512,512]{1,0:T(8,128)(2,1)S(1)} %copy-done.2, ...), custom_call_target="tpu_custom_call" | custom-call | tf_op jit(solution)/shard_map/pallas_call | solution.py:386
  94.4 0.0 copy-start
  94.4 2.2 %copy-done = bf16[512,4096]{1,0:T(8,128)(2,1)S(1)} copy-done((bf16[512,4096]{1,0:T(8,128)(2,1)S(1)}, bf16[512,4096]{1,0:T(8,128)(2,1)}, u32[]{:S(2)}) %copy-start) | copy-done | bytes 4194328
  96.6 30.8 %shard_map.83 = bf16[512,512]{1,0:T(8,128)(2,1)S(1)} custom-call(bf16[512,512]{1,0:T(8,128)(2,1)S(1)} %shard_map.82.att_ref, bf16[512,4096]{1,0:T(8,128)(2,1)S(1)} %copy-done), custom_call_target="tpu_custom_call" | custom-call | tf_op jit(solution)/shard_map/pallas_call | solution.py:419
  127.5 0.8 copy.21
  (5 shorter events, 0.0 us)
Async XLA Ops:
  4.8 1.2 copy-start.1
  6.0 1.0 copy-start.2
  7.0 0.9 copy-start.3
  8.0 0.7 copy-start.4
  94.4 2.2 %copy-start = (bf16[512,4096]{1,0:T(8,128)(2,1)S(1)}, bf16[512,4096]{1,0:T(8,128)(2,1)}, u32[]{:S(2)}) copy-start(bf16[512,4096]{1,0:T(8,128)(2,1)} %w_ref.1) | copy-start | bytes 12582916

commit v3 on v0

v3 whole, which is shorter than its diff:
```python
import math

import jax
import jax.numpy as jnp
from jax import lax
from jax.experimental import pallas as pl
from jax.experimental.pallas import tpu as pltpu
from jax.sharding import PartitionSpec as P

QH = 32
KVH = 8
HD = 128
BLK = 128
NG = 16
NS = 4
TOK = 512
PREFIX_BLOCKS = 512
CHUNKS = TOK // BLK
HEADS = QH // KVH
ROWS = HEADS * BLK
WINDOW = 16
REACH = 13
X_SIZE = 4
Z_SIZE = 8
Y_SIZE = 4
QUARTER = NG * BLK // X_SIZE
HALF = QUARTER // 2
PIECE = QUARTER // Z_SIZE
PREFIX_DEV = 16
FRESH_DEV = 4
COPIES = 80
LOADS = 14
OFF = -1e30
EXP_SCALE = math.log2(math.e) / math.sqrt(HD)
OPEN, SHUT, CAUSAL, FIRST_BAND = 0, 1, 2, 3
BIAS_TILES = FIRST_BAND + HEADS * REACH
MESH = pl.DeviceIdType.MESH
BF16 = jnp.bfloat16
F32 = jnp.float32
TRANSPOSED = (((1,), (1,)), ((), ()))


class Sends:
    def __init__(self, send_sem, recv_sem):
        self.send_sem, self.recv_sem, self.started = send_sem, recv_sem, []

    def start(self, src, dst, device):
        slot = len(self.started)
        copy = pltpu.make_async_remote_copy(
            src_ref=src,
            dst_ref=dst,
            send_sem=self.send_sem.at[slot],
            recv_sem=self.recv_sem.at[slot],
            device_id=device,
            device_id_type=MESH,
        )
        copy.start()
        self.started.append(copy)
        return copy

    def finish(self):
        for copy in self.started:
            copy.wait_send()


def make_bias(starts, widths, first_head, bias):
    rows = lax.broadcasted_iota(jnp.int32, (BLK, BLK), 0)
    cols = lax.broadcasted_iota(jnp.int32, (BLK, BLK), 1)
    bias[OPEN] = jnp.zeros((BLK, BLK), F32)
    bias[SHUT] = jnp.full((BLK, BLK), OFF, F32)
    bias[CAUSAL] = jnp.where(rows >= cols, 0.0, OFF)

    @pl.loop(0, HEADS)
    def per_head(head):
        @pl.loop(0, REACH)
        def per_tile(tile):
            distance = (rows - cols) + tile * BLK
            inside = jnp.zeros((BLK, BLK), jnp.bool_)
            for band in range(NS):
                start = starts[first_head + head, band]
                width = widths[first_head + head, band]
                inside = inside | ((distance >= start) & (distance < start + width))
            bias[FIRST_BAND + head * REACH + tile] = jnp.where(inside, 0.0, OFF)


def make_index(blocks, picks, ctx, tp, index):
    first_own = PREFIX_BLOCKS + ctx * CHUNKS

    @pl.loop(0, HEADS)
    def per_head(head):
        picked = [picks[tp * HEADS + head, slot] == 1 for slot in range(NG)]
        listed = [blocks[tp, slot] for slot in range(NG)]

        @pl.loop(0, CHUNKS)
        def vertical(chunk):
            own = first_own + chunk
            for slot in range(NG):
                seen = jnp.where(listed[slot] < own, OPEN, jnp.where(listed[slot] == own, CAUSAL, SHUT))
                index[chunk, head, slot] = jnp.where(picked[slot], seen, SHUT)

        @pl.loop(0, WINDOW)
        def window(tile):
            block = first_own + tile - (REACH - 1)
            shut = block < PREFIX_BLOCKS
            for slot in range(NG):
                shut = shut | (picked[slot] & (listed[slot] == block))
            for chunk in range(CHUNKS):
                back = chunk + (REACH - 1) - tile
                outside = shut | (back < 0) | (back >= REACH)
                index[chunk, head, NG + tile] = jnp.where(outside, SHUT, FIRST_BAND + head * REACH + back)


def kernel(
    blocks, picks, starts, widths, q_hbm, prefix_hbm, fresh_hbm, w_hbm, out,
    kv_k, kv_v, win, q, w, w_in, mine, far_in, near_in, piece_in, vert, bias, index,
    m_s, l_s, acc_s, s_s, p_s, att, att_in, terms, kept, own_s, far_y, near_y,
    load_sem, send_sem, recv_sem,
):
    ctx = lax.axis_index("ctx")
    tp = lax.axis_index("tp")
    x, z = ctx // Z_SIZE, ctx % Z_SIZE
    y, core = tp // 2, tp % 2
    x_far, x_right, x_left = (x + 2) % X_SIZE, (x + 1) % X_SIZE, (x + 3) % X_SIZE
    y_far, y_right, y_left = (y + 2) % Y_SIZE, (y + 1) % Y_SIZE, (y + 3) % Y_SIZE
    right = (x_right * Z_SIZE + z, tp)
    left = (x_left * Z_SIZE + z, tp)
    along = [(x * Z_SIZE + (z + k) % Z_SIZE, tp) for k in range(1, Z_SIZE)]
    size = X_SIZE * Z_SIZE
    after = ((ctx + 1) % size, tp)
    before = ((ctx + size - 1) % size, tp)
    pair = (ctx, y * 2 + (1 - core))
    up = (ctx, y_right * 2 + core)
    down = (ctx, y_left * 2 + core)
    barrier = pltpu.get_barrier_semaphore()
    partners = [right, left] + along + [after, before, pair, up, down]
    for device in partners:
        pl.semaphore_signal(barrier, inc=1, device_id=device, device_id_type=MESH)

    kv = (kv_k, kv_v)
    loads = []

    def load(src, dst):
        copy = pltpu.make_async_copy(src, dst, load_sem.at[len(loads)])
        copy.start()
        loads.append(copy)
        return copy

    kv_loads = [
        (
            load(prefix_hbm.at[part], kv[part].at[pl.ds(0, PREFIX_DEV)]),
            load(fresh_hbm.at[part], kv[part].at[pl.ds(PREFIX_DEV, FRESH_DEV)]),
        )
        for part in range(2)
    ]
    win_loads = [load(fresh_hbm.at[part], win.at[part, pl.ds(WINDOW - FRESH_DEV, FRESH_DEV)]) for part in range(2)]
    q_load = load(q_hbm, q)
    w_load = load(w_hbm, w)
    sends = Sends(send_sem, recv_sem)

    def rows(start, count):
        return pl.ds(pl.multiple_of(start, PIECE), count)

    def pick(part, quarter):
        for step in range(NG // X_SIZE):
            slot = quarter * (NG // X_SIZE) + step
            block = blocks[tp, slot]
            at_prefix = block - ctx * PREFIX_DEV
            at_fresh = block - PREFIX_BLOCKS - ctx * FRESH_DEV
            in_prefix = (at_prefix >= 0) & (at_prefix < PREFIX_DEV)
            in_fresh = (at_fresh >= 0) & (at_fresh < FRESH_DEV)
            row = jnp.where(in_prefix, at_prefix, jnp.where(in_fresh, PREFIX_DEV + at_fresh, 0))
            value = kv[part][row]
            mine[part, rows(slot * BLK, BLK), :] = jnp.where(in_prefix | in_fresh, value, jnp.zeros_like(value))

    def hand_on(part, age):
        src = WINDOW - FRESH_DEV * (1 + age)
        return sends.start(
            win.at[part, pl.ds(src, FRESH_DEV)], win.at[part, pl.ds(src - FRESH_DEV, FRESH_DEV)], after
        )

    far, near, window, pieces, gathered, spread, relayed = {}, {}, {}, {}, {}, {}, {}
    for part in range(2):
        for copy in kv_loads[part]:
            copy.wait()
        pick(part, x_far)
        if part == 0:
            pl.semaphore_wait(barrier, len(partners))
        far[part] = [
            sends.start(mine.at[part, rows(x_far * QUARTER, HALF), :], far_in.at[part, 0], right),
            sends.start(mine.at[part, rows(x_far * QUARTER + HALF, HALF), :], far_in.at[part, 1], left),
        ]
        pick(part, x_right)
        near[part] = [
            sends.start(
                mine.at[part, rows(x_right * QUARTER + HALF, HALF), :], near_in.at[part, 0, pl.ds(HALF, HALF), :], right
            )
        ]
        pick(part, x_left)
        near[part].append(
            sends.start(mine.at[part, rows(x_left * QUARTER, HALF), :], near_in.at[part, 1, pl.ds(0, HALF), :], left)
        )
        win_loads[part].wait()
        window[part, 0] = hand_on(part, 0)
        pick(part, x)
    weights = [
        sends.start(w_hbm.at[:, pl.ds(pl.multiple_of((to * 2 + 1 - core) * TOK, TOK), TOK)], w_in.at[to], pair)
        for to in range(Y_SIZE)
    ]
    make_bias(starts, widths, tp * HEADS, bias)

    def relay_x(part):
        far[part][0].wait_recv()
        mine[part, rows(x_right * QUARTER, HALF), :] += far_in[part, 0]
        near[part].append(
            sends.start(mine.at[part, rows(x_right * QUARTER, HALF), :], near_in.at[part, 0, pl.ds(0, HALF), :], right)
        )
        far[part][1].wait_recv()
        mine[part, rows(x_left * QUARTER + HALF, HALF), :] += far_in[part, 1]
        near[part].append(
            sends.start(
                mine.at[part, rows(x_left * QUARTER + HALF, HALF), :], near_in.at[part, 1, pl.ds(HALF, HALF), :], left
            )
        )

    def scatter_z(part):
        for copy in near[part]:
            copy.wait_recv()
        own = rows(x * QUARTER, QUARTER)
        mine[part, own, :] = mine[part, own, :] + near_in[part, 0] + near_in[part, 1]
        pieces[part] = [
            sends.start(
                mine.at[part, rows(x * QUARTER + (z + k) % Z_SIZE * PIECE, PIECE), :],
                piece_in.at[part, k - 1],
                along[k - 1],
            )
            for k in range(1, Z_SIZE)
        ]

    def gather_z(part):
        at = rows(x * QUARTER + z * PIECE, PIECE)
        total = mine[part, at, :]
        for k in range(1, Z_SIZE):
            pieces[part][k - 1].wait_recv()
            total = total + piece_in[part, k - 1]
        vert[part, at, :] = total
        gathered[part] = [
            sends.start(vert.at[part, at, :], vert.at[part, at, :], along[k - 1]) for k in range(1, Z_SIZE)
        ]

    def spread_x(part):
        for copy in gathered[part]:
            copy.wait_recv()
        spread[part] = []
        for start in (0, HALF):
            at = rows(x * QUARTER + start, HALF)
            for device in (right, left):
                spread[part].append(sends.start(vert.at[part, at, :], vert.at[part, at, :], device))

    def relay_back(part):
        top_right, top_left, low_right, low_left = spread[part]
        top_right.wait_recv()
        at = rows(x_left * QUARTER, HALF)
        relayed[part] = [sends.start(vert.at[part, at, :], vert.at[part, at, :], right)]
        low_left.wait_recv()
        at = rows(x_right * QUARTER + HALF, HALF)
        relayed[part].append(sends.start(vert.at[part, at, :], vert.at[part, at, :], left))

    def complete(part):
        spread[part][1].wait_recv()
        spread[part][2].wait_recv()
        for copy in relayed[part]:
            copy.wait_recv()

    def pass_window(age):
        for part in range(2):
            window[part, age].wait_recv()
            if age < 2:
                window[part, age + 1] = hand_on(part, age + 1)

    def queries(chunk, head):
        return q[pl.ds(pl.multiple_of(chunk * BLK, BLK), BLK), head * HD : (head + 1) * HD]

    def head_rows(head):
        return slice(head * BLK, (head + 1) * BLK)

    def score(chunk, head, keys, tile, column, count, best):
        s = lax.dot_general(queries(chunk, head), keys, TRANSPOSED, preferred_element_type=F32)
        for j in range(count):
            piece = s[:, j * BLK : (j + 1) * BLK] + bias[index[chunk, head, tile + j]]
            s_s[head_rows(head), (column + j) * BLK : (column + j + 1) * BLK] = piece
            best = piece if best is None else jnp.maximum(best, piece)
        return best

    def weigh(head, top, column, count, total):
        probs = []
        for j in range(count):
            piece = s_s[head_rows(head), (column + j) * BLK : (column + j + 1) * BLK]
            piece = jnp.exp2((piece - top) * EXP_SCALE)
            total = piece if total is None else total + piece
            probs.append(piece.astype(BF16))
        return jnp.concatenate(probs, axis=1), total

    def wide(best):
        return jnp.broadcast_to(jnp.max(best, axis=1, keepdims=True), (BLK, BLK))

    def band(chunks, first, count, begin):
        @pl.loop(*chunks)
        def per_chunk(chunk):
            keys = win[0, first : first + count].reshape(count * BLK, HD)
            values = win[1, first : first + count].reshape(count * BLK, HD)
            best = None
            for head in range(HEADS + 1):
                fresh = None
                if head < HEADS:
                    fresh = score(chunk, head, keys, NG + first, 0, count, None)
                if head > 0:
                    done = head_rows(head - 1)
                    top = wide(best)
                    if not begin:
                        top = jnp.maximum(m_s[chunk, done, :], top)
                    probs, total = weigh(head - 1, top, 0, count, None)
                    product = jnp.dot(probs, values, preferred_element_type=F32)
                    if begin:
                        l_s[chunk, done, :] = total
                        acc_s[chunk, done, :] = product
                    else:
                        fade = jnp.exp2((m_s[chunk, done, :] - top) * EXP_SCALE)
                        l_s[chunk, done, :] = l_s[chunk, done, :] * fade + total
                        acc_s[chunk, done, :] = acc_s[chunk, done, :] * fade + product
                    m_s[chunk, done, :] = top
                best = fresh

    def vertical_scores(chunks):
        step = NG // 2

        @pl.loop(*chunks)
        def per_chunk(chunk):
            best = None
            for head in range(HEADS + 1):
                if head > 0:
                    done = head_rows(head - 1)
                    top = jnp.maximum(m_s[chunk, done, :], wide(best))
                    fade = jnp.exp2((m_s[chunk, done, :] - top) * EXP_SCALE)
                    total = l_s[chunk, done, :] * fade
                best = None
                for first in (0, step):
                    if head < HEADS:
                        keys = vert[0, first * BLK : (first + step) * BLK, :]
                        best = score(chunk, head, keys, first, first, step, best)
                    if head > 0:
                        probs, total = weigh(head - 1, top, first, step, total)
                        p_s[chunk, done, first * BLK : (first + step) * BLK] = probs
                if head > 0:
                    acc_s[chunk, done, :] = acc_s[chunk, done, :] * fade
                    l_s[chunk, done, :] = total

    def vertical_values(chunks):
        @pl.loop(*chunks)
        def per_chunk(chunk):
            product = jnp.dot(p_s[chunk], vert[1], preferred_element_type=F32)
            result = (acc_s[chunk] + product) / jnp.sum(l_s[chunk], axis=1, keepdims=True)
            for head in range(HEADS):
                att[pl.ds(pl.multiple_of(chunk * BLK, BLK), BLK), head * HD : (head + 1) * HD] = result[
                    head_rows(head), :
                ].astype(BF16)

    span = TOK // 2
    part_rows = span // 2

    def exchange(half):
        at = pl.ds(half * span, span)
        return sends.start(att.at[at, :], att_in.at[at, :], pair)

    def term(half, to):
        columns = pl.ds(pl.multiple_of((to * 2 + core) * TOK, TOK), TOK)
        at = slice(half * span, (half + 1) * span)
        total = jnp.dot(att[at, :], w[:, columns], preferred_element_type=F32)
        return total + jnp.dot(att_in[at, :], w_in[to], preferred_element_type=F32)

    def cut(half):
        start = half * span
        return pl.ds(start, part_rows), pl.ds(start + part_rows, part_rows)

    far_sum, near_sum = {}, {}

    def project(half):
        top, low = cut(half)
        total = term(half, y_far)
        terms[0, top, :] = total[:part_rows].astype(BF16)
        terms[0, low, :] = total[part_rows:].astype(BF16)
        far_sum[half] = [
            sends.start(terms.at[0, top, :], far_y.at[half, 0], up),
            sends.start(terms.at[0, low, :], far_y.at[half, 1], down),
        ]
        total = term(half, y_right)
        terms[1, low, :] = total[part_rows:].astype(BF16)
        kept[half, 0] = total[:part_rows]
        near_sum[half] = [sends.start(terms.at[1, low, :], near_y.at[0, low, :], up)]
        total = term(half, y_left)
        terms[2, top, :] = total[:part_rows].astype(BF16)
        kept[half, 1] = total[part_rows:]
        near_sum[half].append(sends.start(terms.at[2, top, :], near_y.at[1, top, :], down))

    def project_own(half):
        own_s[half] = term(half, y)

    def relay_y(half):
        top, low = cut(half)
        far_sum[half][0].wait_recv()
        terms[1, top, :] = (kept[half, 0] + far_y[half, 0].astype(F32)).astype(BF16)
        near_sum[half].append(sends.start(terms.at[1, top, :], near_y.at[0, top, :], up))
        far_sum[half][1].wait_recv()
        terms[2, low, :] = (kept[half, 1] + far_y[half, 1].astype(F32)).astype(BF16)
        near_sum[half].append(sends.start(terms.at[2, low, :], near_y.at[1, low, :], down))

    def total_up(half):
        for copy in near_sum[half]:
            copy.wait_recv()
        at = slice(half * span, (half + 1) * span)
        out[at, :] = (own_s[half] + near_y[0, at, :].astype(F32) + near_y[1, at, :].astype(F32)).astype(BF16)

    relay_x(0)
    make_index(blocks, picks, ctx, tp, index)
    relay_x(1)
    scatter_z(0)
    q_load.wait()
    pass_window(0)
    band((0, 2), 8, 8, True)
    scatter_z(1)
    band((2, 4), 8, 8, True)
    gather_z(0)
    pass_window(1)
    gather_z(1)
    band((0, 4), 4, 4, False)
    spread_x(0)
    spread_x(1)
    relay_back(0)
    pass_window(2)
    band((0, 4), 0, 4, False)
    relay_back(1)
    complete(0)
    vertical_scores((0, 4))
    complete(1)
    vertical_values((0, 2))
    first = exchange(0)
    vertical_values((2, 4))
    second = exchange(1)
    w_load.wait()
    for copy in weights:
        copy.wait_recv()
    first.wait_recv()
    project(0)
    second.wait_recv()
    project(1)
    relay_y(0)
    project_own(0)
    relay_y(1)
    project_own(1)
    total_up(0)
    total_up(1)
    sends.finish()


def local(queries, prefix_kv, fresh_kv, group_blocks, head_pick, band_start, band_width, o_weight):
    vmem = pl.BlockSpec(memory_space=pltpu.VMEM)
    smem = pl.BlockSpec(memory_space=pltpu.SMEM)
    hbm = pl.BlockSpec(memory_space=pl.ANY)
    return pl.pallas_call(
        kernel,
        out_shape=jax.ShapeDtypeStruct((TOK, TOK), BF16),
        in_specs=[smem] * 4 + [hbm] * 4,
        out_specs=vmem,
        scratch_shapes=[
            pltpu.VMEM((PREFIX_DEV + FRESH_DEV, BLK, HD), BF16),
            pltpu.VMEM((PREFIX_DEV + FRESH_DEV, BLK, HD), BF16),
            pltpu.VMEM((2, WINDOW, BLK, HD), BF16),
            pltpu.VMEM((TOK, HEADS * HD), BF16),
            pltpu.VMEM((TOK, QH * HD), BF16),
            pltpu.VMEM((Y_SIZE, TOK, TOK), BF16),
            pltpu.VMEM((2, NG * BLK, HD), BF16),
            pltpu.VMEM((2, 2, HALF, HD), BF16),
            pltpu.VMEM((2, 2, QUARTER, HD), BF16),
            pltpu.VMEM((2, Z_SIZE - 1, PIECE, HD), BF16),
            pltpu.VMEM((2, NG * BLK, HD), BF16),
            pltpu.VMEM((BIAS_TILES, BLK, BLK), F32),
            pltpu.SMEM((CHUNKS, HEADS, NG + WINDOW), jnp.int32),
            pltpu.VMEM((CHUNKS, ROWS, BLK), F32),
            pltpu.VMEM((CHUNKS, ROWS, BLK), F32),
            pltpu.VMEM((CHUNKS, ROWS, HD), F32),
            pltpu.VMEM((ROWS, NG * BLK), F32),
            pltpu.VMEM((CHUNKS, ROWS, NG * BLK), BF16),
            pltpu.VMEM((TOK, HEADS * HD), BF16),
            pltpu.VMEM((TOK, HEADS * HD), BF16),
            pltpu.VMEM((3, TOK, TOK), BF16),
            pltpu.VMEM((2, 2, TOK // 4, TOK), F32),
            pltpu.VMEM((2, TOK // 2, TOK), F32),
            pltpu.VMEM((2, 2, TOK // 4, TOK), BF16),
            pltpu.VMEM((2, TOK, TOK), BF16),
            pltpu.SemaphoreType.DMA((LOADS,)),
            pltpu.SemaphoreType.DMA((COPIES,)),
            pltpu.SemaphoreType.DMA((COPIES,)),
        ],
        compiler_params=pltpu.CompilerParams(
            vmem_limit_bytes=56 * 2**20, collective_id=0, has_side_effects=True
        ),
    )(
        group_blocks,
        head_pick,
        band_start,
        band_width,
        queries,
        prefix_kv.reshape(2, PREFIX_DEV, BLK, HD),
        fresh_kv.reshape(2, FRESH_DEV, BLK, HD),
        o_weight,
    )


def solution(mesh):
    return jax.shard_map(
        local,
        mesh=mesh,
        in_specs=(
            P("ctx", "tp"),
            P(None, "ctx", "tp"),
            P(None, "ctx", "tp"),
            P(),
            P(),
            P(),
            P(),
            P("tp", None),
        ),
        out_specs=P("ctx", "tp"),
        check_vma=False,
    )
```

time: 429 us -> 95 us (0.22)
  waiting for transfers between devices: 209 us -> 0 us
  Pallas kernels: 0 us -> 88.8 us
  matrix products: 72.5 us -> 0 us
  other arithmetic: 55.2 us -> 0 us
  loops' own time: 27.5 us -> 0 us
  local copies, waits for them, and re-layouts: 33.1 us -> 5.96 us
  starting transfers between devices: 15 us -> 0 us
  between operations: 13.6 us -> 0.01 us
    psum x1 -> x0, waiting for transfers between devices: 138 us -> none  [local(): lax.psum(per_head_kv, 'ctx').astype(jnp.float32).astype(jnp.bfloat16)]
    pallas_call x0 -> x1, Pallas kernels: none -> 88.8 us  [local(): pl.pallas_call(kernel, out_shape=jax.ShapeDtypeStruct((TOK, TOK), BF16),...]
    dot_general x17 -> x0, matrix products: 72.5 us -> none  [the longest x4 27.1 us: attend_head(): lax.dot_general(query_rows, band_keys, contract, preferred_element_type=j...]
    reduce_scatter x1 -> x0, waiting for transfers between devices: 37.5 us -> none  [local(): lax.psum_scatter(projected.astype(jnp.bfloat16), 'tp', scatter_dimension=...]
    ppermute x3 -> x0, waiting for transfers between devices: 33.2 us -> none  [passed_along(): return lax.ppermute(block, axis, route)]
    reduce_sum x4 -> x0, other arithmetic: 30.9 us -> none  [attend_head(): jnp.sum(band_exp, axis=1, keepdims=True)]
    another operation x1 -> x0, loops' own time: 27.5 us -> none  [local(): attended = lax.map(attend_head, jnp.arange(local_heads, dtype=jnp.int32))]
    slice x12 -> x0, local copies, waits for them, and re-layouts: 15.4 us -> none  [the longest x4 10.1 us: attend_head(): vert_kv[1]]
  transfers between devices with their start and end apart: 5 -> 0, of which waited for: 4 -> 0; matrix products, arithmetic and copies ran while one was open for 0% -> 0% of each run, Pallas kernels for 0% -> 0%
where the time goes in v3:
time: 95 us; the launch traced here: 94.7 us
  Pallas kernels  88.8 us (93%)
  local copies, waits for them, and re-layouts  5.96 us (6%)
    pallas_call x1, Pallas kernels, local(): pl.pallas_call(kernel, out_shape=jax.ShapeDtypeStruct((TOK, TOK), BF16),...  88.8 us
    unnamed x4, local copies, waits for them, and re-layouts  5.96 us

profile of v3, /device:TPU:1, one launch (start us, length us, event | category | flops | bytes accessed | tf_op | source)
XLA Modules:
  0.0 94.7 jit_solution(8059113886932955397)
XLA Ops:
  0.0 1.4 %copy.9.picks = s32[32,16]{1,0:T(8,128)} copy(s32[32,16]{0,1:T(8,128)} %param.12) | data formatting | bytes 4096 | tf_op args[4]
  1.4 1.4 %copy.10.starts = s32[32,4]{1,0:T(8,128)} copy(s32[32,4]{0,1:T(4,128)} %param.13) | data formatting | bytes 1024 | tf_op args[5]
  2.7 1.4 %copy.11.widths = s32[32,4]{1,0:T(8,128)} copy(s32[32,4]{0,1:T(4,128)} %param.14) | data formatting | bytes 1024 | tf_op args[6]
  4.1 88.8 %shard_map.82 = bf16[512,512]{1,0:T(8,128)(2,1)} custom-call(s32[8,16]{1,0:T(8,128)} %blocks.1, s32[32,16]{1,0:T(8,128)} %copy.9.picks, s32[32,4]{1,0:T(8,128)} %copy.10.starts, s32[32,4]{1,0:T(8,128)} %copy.11.widths, bf16[512,512]{1,0:T(8,128)(2,1)} %q_hbm.1, bf16[2,16,128,128]{3,2,1,0:T(8,128)(2,1)} %bitcast.2, bf16[2,4,128,128]{3,2,1,0:T(8,128)(2,1)} %bitcast.3, ...), custom_call_target="tpu_custom_call" | custom-call | tf_op jit(solution)/shard_map/pallas_call | solution.py:468
  92.9 1.9 %copy.13 = bf16[512,512]{1,0:T(8,128)(2,1)} copy(bf16[512,512]{1,0:T(8,128)(2,1)} %shard_map.82) | data formatting | bytes 1048576

commit v4 on v3

--- a/solution.py
+++ b/solution.py
@@ -29,6 +29,7 @@
 PREFIX_DEV = 16
 FRESH_DEV = 4
 COPIES = 80
+WRAP_COLUMN = 0
 LOADS = 14
 OFF = -1e30
 EXP_SCALE = math.log2(math.e) / math.sqrt(HD)
@@ -77,8 +78,8 @@
             distance = (rows - cols) + tile * BLK
             inside = jnp.zeros((BLK, BLK), jnp.bool_)
             for band in range(NS):
-                start = starts[first_head + head, band]
-                width = widths[first_head + head, band]
+                start = starts[band, first_head + head]
+                width = widths[band, first_head + head]
                 inside = inside | ((distance >= start) & (distance < start + width))
             bias[FIRST_BAND + head * REACH + tile] = jnp.where(inside, 0.0, OFF)
 
@@ -88,7 +89,7 @@
 
     @pl.loop(0, HEADS)
     def per_head(head):
-        picked = [picks[tp * HEADS + head, slot] == 1 for slot in range(NG)]
+        picked = [picks[slot, tp * HEADS + head] == 1 for slot in range(NG)]
         listed = [blocks[tp, slot] for slot in range(NG)]
 
         @pl.loop(0, CHUNKS)
@@ -122,6 +123,11 @@
     y, core = tp // 2, tp % 2
     x_far, x_right, x_left = (x + 2) % X_SIZE, (x + 1) % X_SIZE, (x + 3) % X_SIZE
     y_far, y_right, y_left = (y + 2) % Y_SIZE, (y + 1) % Y_SIZE, (y + 3) % Y_SIZE
+    turned = z == WRAP_COLUMN
+    x_a = jnp.where(turned, x_left, x_right)
+    x_b = jnp.where(turned, x_right, x_left)
+    side_a = (x_a * Z_SIZE + z, tp)
+    side_b = (x_b * Z_SIZE + z, tp)
     right = (x_right * Z_SIZE + z, tp)
     left = (x_left * Z_SIZE + z, tp)
     along = [(x * Z_SIZE + (z + k) % Z_SIZE, tp) for k in range(1, Z_SIZE)]
@@ -179,40 +185,27 @@
         )
 
     far, near, window, pieces, gathered, spread, relayed = {}, {}, {}, {}, {}, {}, {}
-    for part in range(2):
-        for copy in kv_loads[part]:
-            copy.wait()
-        pick(part, x_far)
-        if part == 0:
-            pl.semaphore_wait(barrier, len(partners))
+    def far_start(part):
         far[part] = [
-            sends.start(mine.at[part, rows(x_far * QUARTER, HALF), :], far_in.at[part, 0], right),
+            sends.start(mine.at[part, rows(x_far * QUARTER, HALF), :], far_in.at[part, 0], side_a),
             sends.start(mine.at[part, rows(x_far * QUARTER + HALF, HALF), :], far_in.at[part, 1], left),
         ]
+
+    def near_start(part):
         pick(part, x_right)
+        pick(part, x_left)
         near[part] = [
+            sends.start(mine.at[part, rows(x_b * QUARTER, HALF), :], near_in.at[part, 1, pl.ds(0, HALF), :], side_b),
             sends.start(
                 mine.at[part, rows(x_right * QUARTER + HALF, HALF), :], near_in.at[part, 0, pl.ds(HALF, HALF), :], right
-            )
+            ),
         ]
-        pick(part, x_left)
-        near[part].append(
-            sends.start(mine.at[part, rows(x_left * QUARTER, HALF), :], near_in.at[part, 1, pl.ds(0, HALF), :], left)
-        )
-        win_loads[part].wait()
-        window[part, 0] = hand_on(part, 0)
-        pick(part, x)
-    weights = [
-        sends.start(w_hbm.at[:, pl.ds(pl.multiple_of((to * 2 + 1 - core) * TOK, TOK), TOK)], w_in.at[to], pair)
-        for to in range(Y_SIZE)
-    ]
-    make_bias(starts, widths, tp * HEADS, bias)
 
     def relay_x(part):
         far[part][0].wait_recv()
-        mine[part, rows(x_right * QUARTER, HALF), :] += far_in[part, 0]
+        mine[part, rows(x_a * QUARTER, HALF), :] += far_in[part, 0]
         near[part].append(
-            sends.start(mine.at[part, rows(x_right * QUARTER, HALF), :], near_in.at[part, 0, pl.ds(0, HALF), :], right)
+            sends.start(mine.at[part, rows(x_a * QUARTER, HALF), :], near_in.at[part, 0, pl.ds(0, HALF), :], side_a)
         )
         far[part][1].wait_recv()
         mine[part, rows(x_left * QUARTER + HALF, HALF), :] += far_in[part, 1]
@@ -221,6 +214,11 @@
                 mine.at[part, rows(x_left * QUARTER + HALF, HALF), :], near_in.at[part, 1, pl.ds(HALF, HALF), :], left
             )
         )
+
+    def start_window():
+        for part in range(2):
+            win_loads[part].wait()
+            window[part, 0] = hand_on(part, 0)
 
     def scatter_z(part):
         for copy in near[part]:
@@ -250,24 +248,24 @@
     def spread_x(part):
         for copy in gathered[part]:
             copy.wait_recv()
-        spread[part] = []
-        for start in (0, HALF):
-            at = rows(x * QUARTER + start, HALF)
-            for device in (right, left):
-                spread[part].append(sends.start(vert.at[part, at, :], vert.at[part, at, :], device))
+        top = rows(x * QUARTER, HALF)
+        low = rows(x * QUARTER + HALF, HALF)
+        spread[part] = [
+            sends.start(vert.at[part, at, :], vert.at[part, at, :], device)
+            for at, device in ((top, side_a), (low, left), (top, side_b), (low, right))
+        ]
 
     def relay_back(part):
-        top_right, top_left, low_right, low_left = spread[part]
-        top_right.wait_recv()
-        at = rows(x_left * QUARTER, HALF)
-        relayed[part] = [sends.start(vert.at[part, at, :], vert.at[part, at, :], right)]
-        low_left.wait_recv()
+        spread[part][0].wait_recv()
+        at = rows(x_b * QUARTER, HALF)
+        relayed[part] = [sends.start(vert.at[part, at, :], vert.at[part, at, :], side_a)]
+        spread[part][1].wait_recv()
         at = rows(x_right * QUARTER + HALF, HALF)
         relayed[part].append(sends.start(vert.at[part, at, :], vert.at[part, at, :], left))
 
     def complete(part):
-        spread[part][1].wait_recv()
         spread[part][2].wait_recv()
+        spread[part][3].wait_recv()
         for copy in relayed[part]:
             copy.wait_recv()
 
@@ -419,25 +417,50 @@
         at = slice(half * span, (half + 1) * span)
         out[at, :] = (own_s[half] + near_y[0, at, :].astype(F32) + near_y[1, at, :].astype(F32)).astype(BF16)
 
+    weights = []
+
+    def start_weights():
+        for to in range(Y_SIZE):
+            columns = pl.ds(pl.multiple_of((to * 2 + 1 - core) * TOK, TOK), TOK)
+            weights.append(sends.start(w_hbm.at[:, columns], w_in.at[to], pair))
+
+    for copy in kv_loads[0]:
+        copy.wait()
+    pick(0, x_far)
+    pl.semaphore_wait(barrier, len(partners))
+    far_start(0)
+    near_start(0)
+    for copy in kv_loads[1]:
+        copy.wait()
+    pick(1, x_far)
+    far_start(1)
+    start_window()
+    pick(0, x)
     relay_x(0)
+    near_start(1)
+    pick(1, x)
+    relay_x(1)
+    start_weights()
+    make_bias(starts, widths, tp * HEADS, bias)
+    scatter_z(0)
     make_index(blocks, picks, ctx, tp, index)
-    relay_x(1)
-    scatter_z(0)
     q_load.wait()
+    scatter_z(1)
     pass_window(0)
     band((0, 2), 8, 8, True)
-    scatter_z(1)
-    band((2, 4), 8, 8, True)
     gather_z(0)
+    band((2, 3), 8, 8, True)
+    gather_z(1)
     pass_window(1)
-    gather_z(1)
-    band((0, 4), 4, 4, False)
+    band((3, 4), 8, 8, True)
+    band((0, 2), 4, 4, False)
     spread_x(0)
+    band((2, 4), 4, 4, False)
     spread_x(1)
     relay_back(0)
     pass_window(2)
+    relay_back(1)
     band((0, 4), 0, 4, False)
-    relay_back(1)
     complete(0)
     vertical_scores((0, 4))
     complete(1)
@@ -505,9 +528,9 @@
         ),
     )(
         group_blocks,
-        head_pick,
-        band_start,
-        band_width,
+        head_pick.T,
+        band_start.T,
+        band_width.T,
         queries,
         prefix_kv.reshape(2, PREFIX_DEV, BLK, HD),
         fresh_kv.reshape(2, FRESH_DEV, BLK, HD),

time: 95 us -> 82.7 us (0.87)
  Pallas kernels: 88.8 us -> 80.6 us
  local copies, waits for them, and re-layouts: 5.96 us -> 1.87 us
    pallas_call x1, Pallas kernels: 88.8 us -> 80.6 us  [local(): pl.pallas_call(kernel, out_shape=jax.ShapeDtypeStruct((TOK, TOK), BF16),...]
    unnamed x4 -> x1, local copies, waits for them, and re-layouts: 5.96 us -> 1.87 us
where the time goes in v4:
time: 82.7 us; the launch traced here: 82.5 us
  Pallas kernels  80.6 us (97%)
  local copies, waits for them, and re-layouts  1.87 us (2%)
    pallas_call x1, Pallas kernels, local(): pl.pallas_call(kernel, out_shape=jax.ShapeDtypeStruct((TOK, TOK), BF16),...  80.6 us
    unnamed x1, local copies, waits for them, and re-layouts  1.87 us

profile of v4, /device:TPU:1, one launch (start us, length us, event | category | flops | bytes accessed | tf_op | source)
XLA Modules:
  0.0 82.5 jit_solution(16775733248183157886)
XLA Ops:
  0.0 80.6 %shard_map.82 = bf16[512,512]{1,0:T(8,128)(2,1)} custom-call(s32[8,16]{1,0:T(8,128)} %blocks.1, s32[16,32]{1,0:T(8,128)} %bitcast.7, s32[4,32]{1,0:T(4,128)} %bitcast.8, s32[4,32]{1,0:T(4,128)} %bitcast.9, bf16[512,512]{1,0:T(8,128)(2,1)} %q_hbm.1, bf16[2,16,128,128]{3,2,1,0:T(8,128)(2,1)} %bitcast.5, bf16[2,4,128,128]{3,2,1,0:T(8,128)(2,1)} %bitcast.6, ...), custom_call_target="tpu_custom_call" | custom-call | tf_op jit(solution)/shard_map/pallas_call | solution.py:491
  80.6 1.9 %copy.10 = bf16[512,512]{1,0:T(8,128)(2,1)} copy(bf16[512,512]{1,0:T(8,128)(2,1)} %shard_map.82) | data formatting | bytes 1048576

commit v5 on v4

--- a/solution.py
+++ b/solution.py
@@ -28,7 +28,8 @@
 PIECE = QUARTER // Z_SIZE
 PREFIX_DEV = 16
 FRESH_DEV = 4
-COPIES = 80
+COPIES = 96
+UNITS = 4
 WRAP_COLUMN = 0
 LOADS = 14
 OFF = -1e30
@@ -362,7 +363,7 @@
                     head_rows(head), :
                 ].astype(BF16)
 
-    span = TOK // 2
+    span = TOK // UNITS
     part_rows = span // 2
 
     def exchange(half):
@@ -462,25 +463,41 @@
     relay_back(1)
     band((0, 4), 0, 4, False)
     complete(0)
-    vertical_scores((0, 4))
+    vertical_scores((0, 1))
     complete(1)
-    vertical_values((0, 2))
-    first = exchange(0)
-    vertical_values((2, 4))
-    second = exchange(1)
+    swapped = {}
+
+    def values(unit):
+        vertical_values((unit, unit + 1))
+        swapped[unit] = exchange(unit)
+
+    values(0)
+    vertical_scores((1, 2))
+    values(1)
     w_load.wait()
     for copy in weights:
         copy.wait_recv()
-    first.wait_recv()
+    swapped[0].wait_recv()
     project(0)
-    second.wait_recv()
+    vertical_scores((2, 3))
+    values(2)
+    swapped[1].wait_recv()
     project(1)
     relay_y(0)
+    vertical_scores((3, 4))
+    values(3)
+    swapped[2].wait_recv()
+    project(2)
+    relay_y(1)
+    swapped[3].wait_recv()
+    project(3)
+    relay_y(2)
     project_own(0)
-    relay_y(1)
-    project_own(1)
-    total_up(0)
-    total_up(1)
+    relay_y(3)
+    for unit in range(1, UNITS):
+        project_own(unit)
+    for unit in range(UNITS):
+        total_up(unit)
     sends.finish()
 
 
@@ -515,9 +532,9 @@
             pltpu.VMEM((TOK, HEADS * HD), BF16),
             pltpu.VMEM((TOK, HEADS * HD), BF16),
             pltpu.VMEM((3, TOK, TOK), BF16),
-            pltpu.VMEM((2, 2, TOK // 4, TOK), F32),
-            pltpu.VMEM((2, TOK // 2, TOK), F32),
-            pltpu.VMEM((2, 2, TOK // 4, TOK), BF16),
+            pltpu.VMEM((UNITS, 2, TOK // UNITS // 2, TOK), F32),
+            pltpu.VMEM((UNITS, TOK // UNITS, TOK), F32),
+            pltpu.VMEM((UNITS, 2, TOK // UNITS // 2, TOK), BF16),
             pltpu.VMEM((2, TOK, TOK), BF16),
             pltpu.SemaphoreType.DMA((LOADS,)),
             pltpu.SemaphoreType.DMA((COPIES,)),

time: 82.7 us -> 77.1 us (0.932)
  Pallas kernels: 80.6 us -> 75 us
    pallas_call x1, Pallas kernels: 80.6 us -> 75 us  [local(): pl.pallas_call(kernel, out_shape=jax.ShapeDtypeStruct((TOK, TOK), BF16),...]
where the time goes in v5:
time: 77.1 us; the launch traced here: 76.9 us
  Pallas kernels  75 us (97%)
  local copies, waits for them, and re-layouts  1.87 us (2%)
    pallas_call x1, Pallas kernels, local(): pl.pallas_call(kernel, out_shape=jax.ShapeDtypeStruct((TOK, TOK), BF16),...  75 us
    unnamed x1, local copies, waits for them, and re-layouts  1.87 us

profile of v5, /device:TPU:1, one launch (start us, length us, event | category | flops | bytes accessed | tf_op | source)
XLA Modules:
  0.0 76.9 jit_solution(12159210270171719119)
XLA Ops:
  0.0 75.0 %shard_map.82 = bf16[512,512]{1,0:T(8,128)(2,1)} custom-call(s32[8,16]{1,0:T(8,128)} %blocks.1, s32[16,32]{1,0:T(8,128)} %bitcast.7, s32[4,32]{1,0:T(4,128)} %bitcast.8, s32[4,32]{1,0:T(4,128)} %bitcast.9, bf16[512,512]{1,0:T(8,128)(2,1)} %q_hbm.1, bf16[2,16,128,128]{3,2,1,0:T(8,128)(2,1)} %bitcast.5, bf16[2,4,128,128]{3,2,1,0:T(8,128)(2,1)} %bitcast.6, ...), custom_call_target="tpu_custom_call" | custom-call | tf_op jit(solution)/shard_map/pallas_call | solution.py:508
  75.0 1.9 %copy.10 = bf16[512,512]{1,0:T(8,128)(2,1)} copy(bf16[512,512]{1,0:T(8,128)(2,1)} %shard_map.82) | data formatting | bytes 1048576

commit v6 on v5

--- a/solution.py
+++ b/solution.py
@@ -116,7 +116,7 @@
     blocks, picks, starts, widths, q_hbm, prefix_hbm, fresh_hbm, w_hbm, out,
     kv_k, kv_v, win, q, w, w_in, mine, far_in, near_in, piece_in, vert, bias, index,
     m_s, l_s, acc_s, s_s, p_s, att, att_in, terms, kept, own_s, far_y, near_y,
-    load_sem, send_sem, recv_sem,
+    load_sem, send_sem, recv_sem, reached,
 ):
     ctx = lax.axis_index("ctx")
     tp = lax.axis_index("tp")
@@ -139,7 +139,8 @@
     up = (ctx, y_right * 2 + core)
     down = (ctx, y_left * 2 + core)
     barrier = pltpu.get_barrier_semaphore()
-    partners = [right, left] + along + [after, before, pair, up, down]
+    two_on, two_back = along[1], along[Z_SIZE - 3]
+    partners = [right, left, along[0], two_on, two_back, along[Z_SIZE - 2], after, before, pair, up, down]
     for device in partners:
         pl.semaphore_signal(barrier, inc=1, device_id=device, device_id_type=MESH)
 
@@ -429,6 +430,8 @@
         copy.wait()
     pick(0, x_far)
     pl.semaphore_wait(barrier, len(partners))
+    for device in (two_on, two_back):
+        pl.semaphore_signal(reached, inc=1, device_id=device, device_id_type=MESH)
     far_start(0)
     near_start(0)
     for copy in kv_loads[1]:
@@ -443,10 +446,11 @@
     relay_x(1)
     start_weights()
     make_bias(starts, widths, tp * HEADS, bias)
+    pl.semaphore_wait(reached, 2)
     scatter_z(0)
-    make_index(blocks, picks, ctx, tp, index)
     q_load.wait()
     scatter_z(1)
+    make_index(blocks, picks, ctx, tp, index)
     pass_window(0)
     band((0, 2), 8, 8, True)
     gather_z(0)
@@ -539,6 +543,7 @@
             pltpu.SemaphoreType.DMA((LOADS,)),
             pltpu.SemaphoreType.DMA((COPIES,)),
             pltpu.SemaphoreType.DMA((COPIES,)),
+            pltpu.SemaphoreType.REGULAR,
         ],
         compiler_params=pltpu.CompilerParams(
             vmem_limit_bytes=56 * 2**20, collective_id=0, has_side_effects=True

time: 77.1 us -> 76.3 us (0.990)
  Pallas kernels: 75 us -> 73.8 us
    pallas_call x1, Pallas kernels: 75 us -> 73.8 us  [local(): pl.pallas_call(kernel, out_shape=jax.ShapeDtypeStruct((TOK, TOK), BF16),...]
where the time goes in v6:
time: 76.3 us; the launch traced here: 75.7 us
  Pallas kernels  73.8 us (97%)
  local copies, waits for them, and re-layouts  1.87 us (2%)
    pallas_call x1, Pallas kernels, local(): pl.pallas_call(kernel, out_shape=jax.ShapeDtypeStruct((TOK, TOK), BF16),...  73.8 us
    unnamed x1, local copies, waits for them, and re-layouts  1.87 us

profile of v6, /device:TPU:1, one launch (start us, length us, event | category | flops | bytes accessed | tf_op | source)
XLA Modules:
  0.0 75.7 jit_solution(4827205820545256748)
XLA Ops:
  0.0 73.8 %shard_map.82 = bf16[512,512]{1,0:T(8,128)(2,1)} custom-call(s32[8,16]{1,0:T(8,128)} %blocks.1, s32[16,32]{1,0:T(8,128)} %bitcast.7, s32[4,32]{1,0:T(4,128)} %bitcast.8, s32[4,32]{1,0:T(4,128)} %bitcast.9, bf16[512,512]{1,0:T(8,128)(2,1)} %q_hbm.1, bf16[2,16,128,128]{3,2,1,0:T(8,128)(2,1)} %bitcast.5, bf16[2,4,128,128]{3,2,1,0:T(8,128)(2,1)} %bitcast.6, ...), custom_call_target="tpu_custom_call" | custom-call | tf_op jit(solution)/shard_map/pallas_call | solution.py:512
  73.9 1.9 %copy.10 = bf16[512,512]{1,0:T(8,128)(2,1)} copy(bf16[512,512]{1,0:T(8,128)(2,1)} %shard_map.82) | data formatting | bytes 1048576

commit v7 on v6

--- a/solution.py
+++ b/solution.py
@@ -129,6 +129,9 @@
     x_b = jnp.where(turned, x_right, x_left)
     side_a = (x_a * Z_SIZE + z, tp)
     side_b = (x_b * Z_SIZE + z, tp)
+    x_back = x_left
+    back_a = (x_right * Z_SIZE + z, tp)
+    back_b = (x_left * Z_SIZE + z, tp)
     right = (x_right * Z_SIZE + z, tp)
     left = (x_left * Z_SIZE + z, tp)
     along = [(x * Z_SIZE + (z + k) % Z_SIZE, tp) for k in range(1, Z_SIZE)]
@@ -254,13 +257,13 @@
         low = rows(x * QUARTER + HALF, HALF)
         spread[part] = [
             sends.start(vert.at[part, at, :], vert.at[part, at, :], device)
-            for at, device in ((top, side_a), (low, left), (top, side_b), (low, right))
+            for at, device in ((top, back_a), (low, left), (top, back_b), (low, right))
         ]
 
     def relay_back(part):
         spread[part][0].wait_recv()
-        at = rows(x_b * QUARTER, HALF)
-        relayed[part] = [sends.start(vert.at[part, at, :], vert.at[part, at, :], side_a)]
+        at = rows(x_back * QUARTER, HALF)
+        relayed[part] = [sends.start(vert.at[part, at, :], vert.at[part, at, :], back_a)]
         spread[part][1].wait_recv()
         at = rows(x_right * QUARTER + HALF, HALF)
         relayed[part].append(sends.start(vert.at[part, at, :], vert.at[part, at, :], left))

time: 76.3 us -> 80.1 us (1.050)
  Pallas kernels: 73.8 us -> 78.1 us
    pallas_call x1, Pallas kernels: 73.8 us -> 78.1 us  [local(): pl.pallas_call(kernel, out_shape=jax.ShapeDtypeStruct((TOK, TOK), BF16),...]
where the time goes in v7:
time: 80.1 us; the launch traced here: 79.9 us
  Pallas kernels  78.1 us (98%)
  local copies, waits for them, and re-layouts  1.87 us (2%)
    pallas_call x1, Pallas kernels, local(): pl.pallas_call(kernel, out_shape=jax.ShapeDtypeStruct((TOK, TOK), BF16),...  78.1 us
    unnamed x1, local copies, waits for them, and re-layouts  1.87 us

profile of v7, /device:TPU:1, one launch (start us, length us, event | category | flops | bytes accessed | tf_op | source)
XLA Modules:
  0.0 79.9 jit_solution(18325107960720446874)
XLA Ops:
  0.0 78.1 %shard_map.82 = bf16[512,512]{1,0:T(8,128)(2,1)} custom-call(s32[8,16]{1,0:T(8,128)} %blocks.1, s32[16,32]{1,0:T(8,128)} %bitcast.7, s32[4,32]{1,0:T(4,128)} %bitcast.8, s32[4,32]{1,0:T(4,128)} %bitcast.9, bf16[512,512]{1,0:T(8,128)(2,1)} %q_hbm.1, bf16[2,16,128,128]{3,2,1,0:T(8,128)(2,1)} %bitcast.5, bf16[2,4,128,128]{3,2,1,0:T(8,128)(2,1)} %bitcast.6, ...), custom_call_target="tpu_custom_call" | custom-call | tf_op jit(solution)/shard_map/pallas_call | solution.py:515
  78.1 1.9 %copy.10 = bf16[512,512]{1,0:T(8,128)(2,1)} copy(bf16[512,512]{1,0:T(8,128)(2,1)} %shard_map.82) | data formatting | bytes 1048576
